TPU v7x, 32 devices: a whole 2x2x4 slice. The times are simulated.
32 devices in a mesh: user: 8 (over z, x), tp: 4 (over y, core).
Axes of the slice: x: 2, y: 2, z: 4, core: 2. Of those that a mesh axis runs over, the one named last changes fastest.
Arguments:
- cand_feats: bfloat16 [8192, 1024], P('user', 'tp'), may hold values from -6 to 6
- w_in: bfloat16 [1024, 2048], P(None, 'tp'), may hold values from -0.1875 to 0.1875
- w_out: bfloat16 [1024, 1024], P('tp'), may hold values from -0.1875 to 0.1875
- kv_cache: bfloat16 [512, 128, 2048], P('user', None, 'tp'), may hold values from -6 to 6
- event_mask: int32 [512, 128], P('user'), may hold values from 0 to 1, as said below
- block_counts: int32 [64], P('user'), may hold values from 1 to 8, as said below
- user_blocks: int32 [64, 8], P('user'), may hold values from 0 to 63, as said below
- send_slots: int32 [64, 8], P('user'), may hold values from 0 to 63, as said below
- cand_user: int32 [8192], P('user'), may hold values from 0 to 7
Outputs:
- scored: bfloat16 [8192, 1024], P('user', 'tp')
Inputs may be any that keep to these rules, and one draw needn't show every extreme that they name: `block_counts`: on every index of the user axis some user has 8 blocks, and on one index every user has. For user u of the index r of the user axis and j < block_counts[r * 8 + u], user_blocks[r * 8 + u, j] = o * 8 + c says that block j of u's history is cached on index o, in its local row send_slots[o * 8 + r, c] of kv_cache and event_mask. These valid entries of one index's users are all different, and on one index they take all 64 values. Entries with j >= block_counts[u] are arbitrary. `send_slots`: the 8 rows of one holder o (rows o * 8 to o * 8 + 7) name each of its local rows 0 to 63 exactly once. `event_mask`: in every block of a user's history the first event is real.
All inputs are finite; a program needn't handle non-finite values.
Results may differ from a plain program's by a relative error of at most 0.013.
Values may be sent and summed in bfloat16 or wider, within the bound.
No kernel may reach another device: no remote copies, remote signals or barrier semaphores. Data moves between devices by JAX's collectives and lax.ppermute only.
A program may use at most 128 MiB of HBM per device.

v0:
```python
import functools

import jax
import jax.numpy as jnp
from jax import lax
from jax.experimental import pallas as pl
from jax.experimental.pallas import tpu as pltpu
from jax.sharding import PartitionSpec as P

DH = 128
EVENTS = 128
norm_eps = 1e-06
MASKED = -1e30

VMEM = pl.BlockSpec(memory_space=pltpu.VMEM)
SMEM = pl.BlockSpec(memory_space=pltpu.SMEM)


def pinned(*values):
    return [pltpu.with_memory_space_constraint(value, pltpu.VMEM) for value in values]


def ring_order(count):
    wide = 1
    while 4 * wide * wide <= count:
        wide *= 2
    deep = count // wide
    order = [z * wide for z in range(deep)]
    for turn, z in enumerate(reversed(range(deep))):
        across = range(1, wide) if turn % 2 == 0 else reversed(range(1, wide))
        order += [z * wide + x for x in across]
    return order


def owner_users(block_count, block_table, slot_count):
    user_count, most_blocks = block_table.shape
    live_mask = jnp.arange(most_blocks, dtype=jnp.int32)[None, :] < block_count[:, None]
    slot_hit = (
        block_table[:, :, None] == jnp.arange(slot_count, dtype=jnp.int32)[None, None, :]
    ) & live_mask[:, :, None]
    user_label = jnp.arange(user_count, dtype=jnp.int32)[:, None, None] + 1
    return jnp.sum(jnp.where(slot_hit, user_label, 0), axis=(0, 1)) - 1


def silu(value):
    return value * (0.5 + 0.5 * jnp.tanh(0.5 * value))


def project_kernel(heads, gate, part, *refs):
    *slices, w_in, out = refs
    width = slices[0].shape[1]
    for h in range(heads):
        column = (2 * h + gate) * DH
        total = None
        for m, piece in enumerate(slices):
            start = pl.multiple_of((part[0] ^ m) * width, width)
            term = jnp.dot(
                piece[...],
                w_in[pl.ds(start, width), column : column + DH],
                preferred_element_type=jnp.float32,
            )
            total = term if total is None else total + term
        out[:, h * DH : (h + 1) * DH] = silu(total).astype(jnp.bfloat16)


def project(part, slices, w_in, heads, gate):
    rows, width = slices[0].shape
    return pl.pallas_call(
        functools.partial(project_kernel, heads, gate),
        out_shape=jax.ShapeDtypeStruct((rows, heads * DH), jnp.bfloat16),
        in_specs=[SMEM] + [VMEM] * (len(slices) + 1),
        out_specs=VMEM,
        compiler_params=pltpu.CompilerParams(vmem_limit_bytes=16 * 1024 * 1024),
        cost_estimate=pl.CostEstimate(
            flops=2 * rows * width * len(slices) * heads * DH,
            bytes_accessed=2 * rows * width * len(slices),
            transcendentals=rows * heads * DH,
        ),
        name="gates" if gate else "queries",
    )(part, *pinned(*slices, w_in))


def attend_kernel(heads, cap, table, q_a, q_b, onehot, penalty, cache, out_a, out_b):
    rows = q_a.shape[0]
    per = min(2, cap)
    for d, (q, out) in enumerate(((q_a, out_a), (q_b, out_b))):
        index = table[d]
        hot = onehot[index, d * rows : (d + 1) * rows]
        for h in range(heads):
            left = jnp.concatenate([q[:, h * DH : (h + 1) * DH], hot], axis=1)
            total = None
            for c in range(0, cap, per):
                held = [cache.at[table[2 + d * cap + c + i]] for i in range(per)]
                keys = jnp.concatenate([b[:, 2 * h * DH : (2 * h + 1) * DH] for b in held], axis=0)
                values = jnp.concatenate(
                    [b[:, (2 * h + 1) * DH : (2 * h + 2) * DH] for b in held], axis=0
                )
                right = jnp.concatenate(
                    [keys, penalty[index, c * EVENTS : (c + per) * EVENTS]], axis=1
                )
                half = lax.dot_general(
                    left, right, (((1,), (1,)), ((), ())), preferred_element_type=jnp.float32
                ) * (0.5 * DH ** (-0.5))
                weights = (half + half * jnp.tanh(half)).astype(jnp.bfloat16)
                term = jnp.dot(weights, values, preferred_element_type=jnp.float32)
                total = term if total is None else total + term
            out[:, h * DH : (h + 1) * DH] = total


def attend(table, q_a, q_b, onehot, penalty, cache, heads, cap):
    rows = q_a.shape[0]
    events = cap * EVENTS
    out = jax.ShapeDtypeStruct((rows, heads * DH), jnp.float32)
    return pl.pallas_call(
        functools.partial(attend_kernel, heads, cap),
        out_shape=(out, out),
        in_specs=[SMEM] + [VMEM] * 5,
        out_specs=(VMEM, VMEM),
        compiler_params=pltpu.CompilerParams(vmem_limit_bytes=16 * 1024 * 1024),
        cost_estimate=pl.CostEstimate(
            flops=2 * 2 * 3 * rows * events * heads * DH,
            bytes_accessed=2 * (events * heads * 4 * DH + events * 2 * DH + rows * heads * DH * 6),
            transcendentals=2 * rows * events * heads,
        ),
        name="attend",
    )(table, *pinned(q_a, q_b, onehot, penalty, cache))


def finish_kernel(heads, parts, part, own, arrived, gates, w_out, sent, kept):
    columns = []
    for h in range(heads):
        at = slice(h * DH, (h + 1) * DH)
        value = own[:, at] + arrived[:, at].astype(jnp.float32)
        scale = lax.rsqrt(jnp.mean(value * value, axis=1, keepdims=True) + norm_eps)
        columns.append((value * scale * gates[:, at].astype(jnp.float32)).astype(jnp.bfloat16))
    hidden = jnp.concatenate(columns, axis=1)
    width = w_out.shape[1] // parts
    for m in range(parts):
        start = pl.multiple_of((part[0] ^ m) * width, width)
        term = jnp.dot(hidden, w_out[:, pl.ds(start, width)], preferred_element_type=jnp.float32)
        if m % 2:
            sent[m // 2] = term.astype(jnp.bfloat16)
        else:
            kept[m // 2] = term


def finish(part, own, arrived, gates, w_out, heads, parts):
    rows = own.shape[0]
    width = w_out.shape[1] // parts
    return pl.pallas_call(
        functools.partial(finish_kernel, heads, parts),
        out_shape=(
            jax.ShapeDtypeStruct((parts // 2, rows, width), jnp.bfloat16),
            jax.ShapeDtypeStruct((parts // 2, rows, width), jnp.float32),
        ),
        in_specs=[SMEM] + [VMEM] * 4,
        out_specs=(VMEM, VMEM),
        compiler_params=pltpu.CompilerParams(vmem_limit_bytes=16 * 1024 * 1024),
        cost_estimate=pl.CostEstimate(
            flops=2 * rows * heads * DH * width * parts,
            bytes_accessed=rows * width * parts * 3,
            transcendentals=rows,
        ),
        name="finish",
    )(part, *pinned(own, arrived, gates, w_out))


def per_device(
    cand_feats, w_in, w_out, kv_cache, event_mask, block_counts, user_blocks, send_slots, cand_user
):
    row_count, slice_width = cand_feats.shape
    heads = w_out.shape[0] // DH
    peers = lax.axis_size("user")
    parts = lax.axis_size("tp")
    cap = send_slots.shape[1]
    me = lax.axis_index("user")
    part = lax.axis_index("tp")
    part_ref = part.reshape(1)
    half = row_count // 2

    order = ring_order(peers)
    place = [0] * peers
    for position, index in enumerate(order):
        place[index] = position
    here = jnp.array(place, jnp.int32)[me]
    onward = [(order[i], order[(i + 1) % peers]) for i in range(peers)]
    back = [(b, a) for a, b in onward]

    def swap(value, axis, bit):
        return lax.ppermute(value, axis, [(i, i ^ bit) for i in range(lax.axis_size(axis))])

    def bits(count):
        return [1 << b for b in range(count.bit_length() - 1)]

    slices = {0: cand_feats}
    for bit in reversed(bits(parts)):
        slices.update({m | bit: swap(value, "tp", bit) for m, value in list(slices.items())})
    slices = [slices[m] for m in range(parts)]

    slot_users = owner_users(block_counts, user_blocks, peers * cap)
    facts = jnp.concatenate([cand_user, slot_users])[None]
    for bit in bits(peers):
        facts = jnp.concatenate([facts, swap(facts, "user", bit)], axis=0)
    users, owners = facts[:, :row_count], facts[:, row_count:]
    labels = jnp.arange(DH, dtype=jnp.int32)
    onehot = (users[:, :, None] == labels).astype(jnp.bfloat16)
    steps = jnp.arange(peers, dtype=jnp.int32)
    slots = send_slots[me ^ steps]
    live = event_mask[slots.reshape(-1)].reshape(peers, cap, EVENTS) > 0
    my_owners = lax.dynamic_slice_in_dim(owners, me * cap, cap, 1)
    label = jnp.where(live, my_owners[:, :, None], -1).reshape(peers, cap * EVENTS)
    penalty = jnp.where(label[:, :, None] == labels, 0.0, MASKED).astype(jnp.bfloat16)

    sequence = jnp.array(order, jnp.int32)
    met = jnp.stack([sequence[(here - steps) % peers], sequence[(here + steps) % peers]], axis=1)
    tables = jnp.concatenate([met ^ me, send_slots[met].reshape(peers, 2 * cap)], axis=1)

    queries = project(part_ref, slices, w_in, heads, 0)
    gates = project(part_ref, slices, w_in, heads, 1)

    def score(step, q_a, q_b):
        return attend(tables[step], q_a, q_b, onehot, penalty, kv_cache, heads, cap)

    q_a, q_b = queries[:half], queries[half:]
    own_a, own_b = score(0, q_a, q_b)
    tables, own_a, own_b = lax.optimization_barrier((tables, own_a, own_b))
    sum_a = sum_b = None
    for step in range(1, peers):
        q_a = lax.ppermute(q_a, "user", onward)
        q_b = lax.ppermute(q_b, "user", back)
        term_a, term_b = score(step, q_a, q_b)
        if sum_a is not None:
            term_a += sum_a.astype(jnp.float32)
            term_b += sum_b.astype(jnp.float32)
        sum_a = lax.ppermute(term_a.astype(jnp.bfloat16), "user", onward)
        sum_b = lax.ppermute(term_b.astype(jnp.bfloat16), "user", back)

    scored = []
    for own, arrived, begin in ((own_a, sum_a, 0), (own_b, sum_b, half)):
        rows = slice(begin, begin + half)
        sent, kept = finish(part_ref, own, arrived, gates[rows], w_out, heads, parts)
        for bit in bits(parts):
            total = kept + swap(sent, "tp", bit).astype(jnp.float32)
            sent, kept = total[1::2].astype(jnp.bfloat16), total[::2]
        scored.append((cand_feats[rows].astype(jnp.float32) + total[0]).astype(jnp.bfloat16))
    return jnp.concatenate(scored, axis=0)


def solution(mesh):
    in_specs = (
        P("user", "tp"),
        P(None, "tp"),
        P("tp", None),
        P("user", None, "tp"),
        P("user", None),
        P("user"),
        P("user", None),
        P("user", None),
        P("user"),
    )
    out_specs = P("user", "tp")
    return jax.shard_map(
        per_device, mesh=mesh, in_specs=in_specs, out_specs=out_specs, check_vma=False
    )
```

profile of v0, /device:TPU:0, one launch (start us, length us, event | category | flops | bytes accessed | tf_op | source)
XLA Modules:
  0.0 140.8 jit_solution(16548061415083312222)
XLA Ops:
  0.0 3.0 %collective-permute-start.1 = (bf16[1024,256]{1,0:T(8,128)(2,1)}, bf16[1024,256]{1,0:T(8,128)(2,1)S(1)}, u32[]{:S(2)}, u32[]{:S(2)}) collective-permute-start(bf16[1024,256]{1,0:T(8,128)(2,1)} %refs_0_.3), channel_id=1, source_target_pairs={{0,2},{1,3},{2,0},{3,1},{4,6},{5,7},{6,4},{7,5},{8,10},{9,11},{10,... | collective-permute-start | bytes 1572872 | tf_op jit(solution)/shard_map/ppermute | solution.py:190
  5.3 1.5 %collective-permute-start.3 = (s32[1,1088]{1,0:T(1,128)S(1)}, s32[1,1088]{1,0:T(1,128)S(1)}, u32[]{:S(2)}, u32[]{:S(2)}) collective-permute-start(s32[1,1088]{1,0:T(1,128)S(1)} %broadcast_in_dim.54), channel_id=1, source_target_pairs={{0,4},{4,0},{8,12},{12,8},{16,20},{20,16},{24,28},{28,24},{1,5},{5... | collective-permute-start | bytes 13064 | tf_op jit(solution)/shard_map/ppermute | solution.py:190
  8.7 1.2 gather_fusion.3
  10.1 1.3 gather_fusion
  11.4 1.3 gather_fusion.1
  13.6 1.2 gather_fusion.2
  14.9 1.6 %collective-permute-start.4 = (s32[2,1088]{1,0:T(2,128)S(1)}, s32[2,1088]{1,0:T(2,128)S(1)}, u32[]{:S(2)}, u32[]{:S(2)}) collective-permute-start(s32[2,1088]{1,0:T(2,128)S(1)} %pad_add_fusion.2), channel_id=1, source_target_pairs={{0,8},{4,12},{8,0},{12,4},{16,24},{20,28},{24,16},{28,20},{1,9},{5... | collective-permute-start | bytes 26120 | tf_op jit(solution)/shard_map/ppermute | solution.py:190
  16.6 2.0 %collective-permute-done.4 = s32[2,1088]{1,0:T(2,128)S(1)} collective-permute-done((s32[2,1088]{1,0:T(2,128)S(1)}, s32[2,1088]{1,0:T(2,128)S(1)}, u32[]{:S(2)}, u32[]{:S(2)}) %collective-permute-start.4) | collective-permute-done | bytes 8736 | tf_op jit(solution)/shard_map/ppermute | solution.py:190
  18.7 2.7 %collective-permute-start.5 = (s32[4,1088]{1,0:T(4,128)S(1)}, s32[4,1088]{1,0:T(4,128)S(1)}, u32[]{:S(2)}, u32[]{:S(2)}) collective-permute-start(s32[4,1088]{1,0:T(4,128)S(1)} %pad_add_fusion.1), channel_id=1, source_target_pairs={{0,16},{4,20},{8,24},{12,28},{16,0},{20,4},{24,8},{28,12},{1,17},{... | collective-permute-start | bytes 52232 | tf_op jit(solution)/shard_map/ppermute | solution.py:190
  21.3 2.1 %collective-permute-done.5 = s32[4,1088]{1,0:T(4,128)S(1)} collective-permute-done((s32[4,1088]{1,0:T(4,128)S(1)}, s32[4,1088]{1,0:T(4,128)S(1)}, u32[]{:S(2)}, u32[]{:S(2)}) %collective-permute-start.5) | collective-permute-done | bytes 17440 | tf_op jit(solution)/shard_map/ppermute | solution.py:190
  23.7 2.2 %select_convert_fusion.penalty = bf16[8,1024,128]{2,1,0:T(8,128)(2,1)S(1)} fusion(s32[8,1024]{1,0:T(8,128)S(1)} %bitcast_select_fusion), kind=kLoop, calls=%fused_computation.5 | loop fusion | flops 3145728 | bytes 2129920 | tf_op jit(solution)/shard_map/convert_element_type | solution.py:212
  25.9 2.2 %fusion.onehot = bf16[8,1024,128]{2,1,0:T(8,128)(2,1)S(1)} fusion(s32[8,1024]{1,0:T(8,128)S(1)} %slice.98), kind=kLoop, calls=%fused_computation.8 | loop fusion | flops 2097152 | bytes 2129920 | tf_op jit(solution)/shard_map/convert_element_type | solution.py:206
  28.1 1.3 queries.1
  30.0 1.5 %collective-permute-start.6 = (bf16[512,256]{1,0:T(8,128)(2,1)S(1)}, bf16[512,256]{1,0:T(8,128)(2,1)S(1)}, u32[]{:S(2)}, u32[]{:S(2)}) collective-permute-start(bf16[512,256]{1,0:T(8,128)(2,1)S(1)} %get-tuple-element.56.q_a), channel_id=1, source_target_pairs={{0,8},{8,16},{16,24},{24,28},{28,20},{20,12},{12,4},{4,0},{1,9},{9... | collective-permute-start | bytes 786440 | tf_op jit(solution)/shard_map/ppermute | solution.py:229
  31.5 3.2 %attend.8 = (f32[512,256]{1,0:T(8,128)S(1)}, f32[512,256]{1,0:T(8,128)S(1)}) custom-call(s32[18]{0:T(128)S(1)} %slice_bitcast_fusion.7.table, bf16[512,256]{1,0:T(8,128)(2,1)S(1)} %get-tuple-element.56.q_a, bf16[512,256]{1,0:T(8,128)(2,1)S(1)} %get-tuple-element.55.q_b, bf16[8,1024,128]{2,1,0:T(8,128)(2,1)S(1)} %fusion.onehot, ...), custom_call_target="tpu_custom_call" | custom-call | flops 1610612736 | bytes 4194304 | tf_op jit(solution)/shard_map/attend/pallas_call | solution.py:114
  34.7 3.4 %collective-permute-done.13.q_b = bf16[512,256]{1,0:T(8,128)(2,1)S(1)} collective-permute-done((bf16[512,256]{1,0:T(8,128)(2,1)S(1)}, bf16[512,256]{1,0:T(8,128)(2,1)S(1)}, u32[]{:S(2)}, u32[]{:S(2)}) %collective-permute-start.13) | collective-permute-done | bytes 262176 | tf_op jit(solution)/shard_map/ppermute | solution.py:230
  38.7 1.5 %collective-permute-start.7 = (bf16[512,256]{1,0:T(8,128)(2,1)S(1)}, bf16[512,256]{1,0:T(8,128)(2,1)S(1)}, u32[]{:S(2)}, u32[]{:S(2)}) collective-permute-start(bf16[512,256]{1,0:T(8,128)(2,1)S(1)} %collective-permute-done.6.q_a), channel_id=1, source_target_pairs={{0,8},{8,16},{16,24},{24,28},{28,20},{20,12},{12,4},{4,0},{1,9},{9... | collective-permute-start | bytes 786440 | tf_op jit(solution)/shard_map/ppermute | solution.py:229
  40.2 3.2 %attend.15 = (f32[512,256]{1,0:T(8,128)S(1)}, f32[512,256]{1,0:T(8,128)S(1)}) custom-call(s32[18]{0:T(128)S(1)} %get-tuple-element.57.table, bf16[512,256]{1,0:T(8,128)(2,1)S(1)} %collective-permute-done.6.q_a, bf16[512,256]{1,0:T(8,128)(2,1)S(1)} %collective-permute-done.13.q_b, bf16[8,1024,128]{2,1,0:T(8,128)(2,1)S(1)} %fusion.onehot, ...), custom_call_target="tpu_custom_call" | custom-call | flops 1610612736 | bytes 4194304 | tf_op jit(solution)/shard_map/attend/pallas_call | solution.py:114
  44.0 2.8 %collective-permute-done.14.q_b = bf16[512,256]{1,0:T(8,128)(2,1)S(1)} collective-permute-done((bf16[512,256]{1,0:T(8,128)(2,1)S(1)}, bf16[512,256]{1,0:T(8,128)(2,1)S(1)}, u32[]{:S(2)}, u32[]{:S(2)}) %collective-permute-start.14) | collective-permute-done | bytes 262176 | tf_op jit(solution)/shard_map/ppermute | solution.py:230
  47.3 1.5 %collective-permute-start.8 = (bf16[512,256]{1,0:T(8,128)(2,1)S(1)}, bf16[512,256]{1,0:T(8,128)(2,1)S(1)}, u32[]{:S(2)}, u32[]{:S(2)}) collective-permute-start(bf16[512,256]{1,0:T(8,128)(2,1)S(1)} %collective-permute-done.7.q_a), channel_id=1, source_target_pairs={{0,8},{8,16},{16,24},{24,28},{28,20},{20,12},{12,4},{4,0},{1,9},{9... | collective-permute-start | bytes 786440 | tf_op jit(solution)/shard_map/ppermute | solution.py:229
  48.8 3.2 %attend.14 = (f32[512,256]{1,0:T(8,128)S(1)}, f32[512,256]{1,0:T(8,128)S(1)}) custom-call(s32[18]{0:T(128)S(1)} %get-tuple-element.58.table, bf16[512,256]{1,0:T(8,128)(2,1)S(1)} %collective-permute-done.7.q_a, bf16[512,256]{1,0:T(8,128)(2,1)S(1)} %collective-permute-done.14.q_b, bf16[8,1024,128]{2,1,0:T(8,128)(2,1)S(1)} %fusion.onehot, ...), custom_call_target="tpu_custom_call" | custom-call | flops 1610612736 | bytes 4194304 | tf_op jit(solution)/shard_map/attend/pallas_call | solution.py:114
  53.4 1.3 gates.1
  54.7 1.7 %collective-permute-start.20 = (bf16[512,256]{1,0:T(8,128)(2,1)S(1)}, bf16[512,256]{1,0:T(8,128)(2,1)S(1)}, u32[]{:S(2)}, u32[]{:S(2)}) collective-permute-start(bf16[512,256]{1,0:T(8,128)(2,1)S(1)} %convert_element_type.113), channel_id=1, source_target_pairs={{0,8},{8,16},{16,24},{24,28},{28,20},{20,12},{12,4},{4,0},{1,9},{9... | collective-permute-start | bytes 786440 | tf_op jit(solution)/shard_map/ppermute | solution.py:235
  56.4 1.9 %collective-permute-done.15.q_b = bf16[512,256]{1,0:T(8,128)(2,1)S(1)} collective-permute-done((bf16[512,256]{1,0:T(8,128)(2,1)S(1)}, bf16[512,256]{1,0:T(8,128)(2,1)S(1)}, u32[]{:S(2)}, u32[]{:S(2)}) %collective-permute-start.15) | collective-permute-done | bytes 262176 | tf_op jit(solution)/shard_map/ppermute | solution.py:230
  58.9 1.5 %collective-permute-start.9 = (bf16[512,256]{1,0:T(8,128)(2,1)S(1)}, bf16[512,256]{1,0:T(8,128)(2,1)S(1)}, u32[]{:S(2)}, u32[]{:S(2)}) collective-permute-start(bf16[512,256]{1,0:T(8,128)(2,1)S(1)} %collective-permute-done.8.q_a), channel_id=1, source_target_pairs={{0,8},{8,16},{16,24},{24,28},{28,20},{20,12},{12,4},{4,0},{1,9},{9... | collective-permute-start | bytes 786440 | tf_op jit(solution)/shard_map/ppermute | solution.py:229
  60.4 3.2 %attend.13 = (f32[512,256]{1,0:T(8,128)S(1)}, f32[512,256]{1,0:T(8,128)S(1)}) custom-call(s32[18]{0:T(128)S(1)} %get-tuple-element.59.table, bf16[512,256]{1,0:T(8,128)(2,1)S(1)} %collective-permute-done.8.q_a, bf16[512,256]{1,0:T(8,128)(2,1)S(1)} %collective-permute-done.15.q_b, bf16[8,1024,128]{2,1,0:T(8,128)(2,1)S(1)} %fusion.onehot, ...), custom_call_target="tpu_custom_call" | custom-call | flops 1610612736 | bytes 4194304 | tf_op jit(solution)/shard_map/attend/pallas_call | solution.py:114
  64.7 1.5 %collective-permute-start.21 = (bf16[512,256]{1,0:T(8,128)(2,1)S(1)}, bf16[512,256]{1,0:T(8,128)(2,1)S(1)}, u32[]{:S(2)}, u32[]{:S(2)}) collective-permute-start(bf16[512,256]{1,0:T(8,128)(2,1)S(1)} %add_convert_fusion.11), channel_id=1, source_target_pairs={{0,8},{8,16},{16,24},{24,28},{28,20},{20,12},{12,4},{4,0},{1,9},{9... | collective-permute-start | bytes 786440 | tf_op jit(solution)/shard_map/ppermute | solution.py:235
  66.2 3.4 %collective-permute-done.16.q_b = bf16[512,256]{1,0:T(8,128)(2,1)S(1)} collective-permute-done((bf16[512,256]{1,0:T(8,128)(2,1)S(1)}, bf16[512,256]{1,0:T(8,128)(2,1)S(1)}, u32[]{:S(2)}, u32[]{:S(2)}) %collective-permute-start.16) | collective-permute-done | bytes 262176 | tf_op jit(solution)/shard_map/ppermute | solution.py:230
  70.1 1.5 %collective-permute-start.10 = (bf16[512,256]{1,0:T(8,128)(2,1)S(1)}, bf16[512,256]{1,0:T(8,128)(2,1)S(1)}, u32[]{:S(2)}, u32[]{:S(2)}) collective-permute-start(bf16[512,256]{1,0:T(8,128)(2,1)S(1)} %collective-permute-done.9.q_a), channel_id=1, source_target_pairs={{0,8},{8,16},{16,24},{24,28},{28,20},{20,12},{12,4},{4,0},{1,9},{9... | collective-permute-start | bytes 786440 | tf_op jit(solution)/shard_map/ppermute | solution.py:229
  71.6 3.2 %attend.12 = (f32[512,256]{1,0:T(8,128)S(1)}, f32[512,256]{1,0:T(8,128)S(1)}) custom-call(s32[18]{0:T(128)S(1)} %get-tuple-element.60.table, bf16[512,256]{1,0:T(8,128)(2,1)S(1)} %collective-permute-done.9.q_a, bf16[512,256]{1,0:T(8,128)(2,1)S(1)} %collective-permute-done.16.q_b, bf16[8,1024,128]{2,1,0:T(8,128)(2,1)S(1)} %fusion.onehot, ...), custom_call_target="tpu_custom_call" | custom-call | flops 1610612736 | bytes 4194304 | tf_op jit(solution)/shard_map/attend/pallas_call | solution.py:114
  75.9 1.5 %collective-permute-start.22 = (bf16[512,256]{1,0:T(8,128)(2,1)S(1)}, bf16[512,256]{1,0:T(8,128)(2,1)S(1)}, u32[]{:S(2)}, u32[]{:S(2)}) collective-permute-start(bf16[512,256]{1,0:T(8,128)(2,1)S(1)} %add_convert_fusion.10), channel_id=1, source_target_pairs={{0,8},{8,16},{16,24},{24,28},{28,20},{20,12},{12,4},{4,0},{1,9},{9... | collective-permute-start | bytes 786440 | tf_op jit(solution)/shard_map/ppermute | solution.py:235
  77.5 3.4 %collective-permute-done.17.q_b = bf16[512,256]{1,0:T(8,128)(2,1)S(1)} collective-permute-done((bf16[512,256]{1,0:T(8,128)(2,1)S(1)}, bf16[512,256]{1,0:T(8,128)(2,1)S(1)}, u32[]{:S(2)}, u32[]{:S(2)}) %collective-permute-start.17) | collective-permute-done | bytes 262176 | tf_op jit(solution)/shard_map/ppermute | solution.py:230
  81.4 1.5 %collective-permute-start.11 = (bf16[512,256]{1,0:T(8,128)(2,1)S(1)}, bf16[512,256]{1,0:T(8,128)(2,1)S(1)}, u32[]{:S(2)}, u32[]{:S(2)}) collective-permute-start(bf16[512,256]{1,0:T(8,128)(2,1)S(1)} %collective-permute-done.10.q_a), channel_id=1, source_target_pairs={{0,8},{8,16},{16,24},{24,28},{28,20},{20,12},{12,4},{4,0},{1,9},{9... | collective-permute-start | bytes 786440 | tf_op jit(solution)/shard_map/ppermute | solution.py:229
  82.9 3.2 %attend.11 = (f32[512,256]{1,0:T(8,128)S(1)}, f32[512,256]{1,0:T(8,128)S(1)}) custom-call(s32[18]{0:T(128)S(1)} %get-tuple-element.61.table, bf16[512,256]{1,0:T(8,128)(2,1)S(1)} %collective-permute-done.10.q_a, bf16[512,256]{1,0:T(8,128)(2,1)S(1)} %collective-permute-done.17.q_b, bf16[8,1024,128]{2,1,0:T(8,128)(2,1)S(1)} %fusion.onehot, ...), custom_call_target="tpu_custom_call" | custom-call | flops 1610612736 | bytes 4194304 | tf_op jit(solution)/shard_map/attend/pallas_call | solution.py:114
  87.2 1.5 %collective-permute-start.23 = (bf16[512,256]{1,0:T(8,128)(2,1)S(1)}, bf16[512,256]{1,0:T(8,128)(2,1)S(1)}, u32[]{:S(2)}, u32[]{:S(2)}) collective-permute-start(bf16[512,256]{1,0:T(8,128)(2,1)S(1)} %add_convert_fusion.9), channel_id=1, source_target_pairs={{0,8},{8,16},{16,24},{24,28},{28,20},{20,12},{12,4},{4,0},{1,9},{9... | collective-permute-start | bytes 786440 | tf_op jit(solution)/shard_map/ppermute | solution.py:235
  88.7 3.4 %collective-permute-done.18.q_b = bf16[512,256]{1,0:T(8,128)(2,1)S(1)} collective-permute-done((bf16[512,256]{1,0:T(8,128)(2,1)S(1)}, bf16[512,256]{1,0:T(8,128)(2,1)S(1)}, u32[]{:S(2)}, u32[]{:S(2)}) %collective-permute-start.18) | collective-permute-done | bytes 262176 | tf_op jit(solution)/shard_map/ppermute | solution.py:230
  92.6 1.5 %collective-permute-start.12 = (bf16[512,256]{1,0:T(8,128)(2,1)S(1)}, bf16[512,256]{1,0:T(8,128)(2,1)S(1)}, u32[]{:S(2)}, u32[]{:S(2)}) collective-permute-start(bf16[512,256]{1,0:T(8,128)(2,1)S(1)} %collective-permute-done.11.q_a), channel_id=1, source_target_pairs={{0,8},{8,16},{16,24},{24,28},{28,20},{20,12},{12,4},{4,0},{1,9},{9... | collective-permute-start | bytes 786440 | tf_op jit(solution)/shard_map/ppermute | solution.py:229
  94.1 3.2 %attend.10 = (f32[512,256]{1,0:T(8,128)S(1)}, f32[512,256]{1,0:T(8,128)S(1)}) custom-call(s32[18]{0:T(128)S(1)} %get-tuple-element.62.table, bf16[512,256]{1,0:T(8,128)(2,1)S(1)} %collective-permute-done.11.q_a, bf16[512,256]{1,0:T(8,128)(2,1)S(1)} %collective-permute-done.18.q_b, bf16[8,1024,128]{2,1,0:T(8,128)(2,1)S(1)} %fusion.onehot, ...), custom_call_target="tpu_custom_call" | custom-call | flops 1610612736 | bytes 4194304 | tf_op jit(solution)/shard_map/attend/pallas_call | solution.py:114
  98.6 1.5 %collective-permute-start.24 = (bf16[512,256]{1,0:T(8,128)(2,1)S(1)}, bf16[512,256]{1,0:T(8,128)(2,1)S(1)}, u32[]{:S(2)}, u32[]{:S(2)}) collective-permute-start(bf16[512,256]{1,0:T(8,128)(2,1)S(1)} %add_convert_fusion.8), channel_id=1, source_target_pairs={{0,8},{8,16},{16,24},{24,28},{28,20},{20,12},{12,4},{4,0},{1,9},{9... | collective-permute-start | bytes 786440 | tf_op jit(solution)/shard_map/ppermute | solution.py:235
  100.2 3.1 %collective-permute-done.19.q_b = bf16[512,256]{1,0:T(8,128)(2,1)S(1)} collective-permute-done((bf16[512,256]{1,0:T(8,128)(2,1)S(1)}, bf16[512,256]{1,0:T(8,128)(2,1)S(1)}, u32[]{:S(2)}, u32[]{:S(2)}) %collective-permute-start.19) | collective-permute-done | bytes 262176 | tf_op jit(solution)/shard_map/ppermute | solution.py:230
  103.3 3.2 %attend.9 = (f32[512,256]{1,0:T(8,128)S(1)}, f32[512,256]{1,0:T(8,128)S(1)}) custom-call(s32[18]{0:T(128)S(1)} %get-tuple-element.63.table, bf16[512,256]{1,0:T(8,128)(2,1)S(1)} %collective-permute-done.12.q_a, bf16[512,256]{1,0:T(8,128)(2,1)S(1)} %collective-permute-done.19.q_b, bf16[8,1024,128]{2,1,0:T(8,128)(2,1)S(1)} %fusion.onehot, ...), custom_call_target="tpu_custom_call" | custom-call | flops 1610612736 | bytes 4194304 | tf_op jit(solution)/shard_map/attend/pallas_call | solution.py:114
  106.5 1.3 collective-permute-done.34
  108.6 1.5 %collective-permute-start.25 = (bf16[512,256]{1,0:T(8,128)(2,1)S(1)}, bf16[512,256]{1,0:T(8,128)(2,1)S(1)}, u32[]{:S(2)}, u32[]{:S(2)}) collective-permute-start(bf16[512,256]{1,0:T(8,128)(2,1)S(1)} %add_convert_fusion.7), channel_id=1, source_target_pairs={{0,8},{8,16},{16,24},{24,28},{28,20},{20,12},{12,4},{4,0},{1,9},{9... | collective-permute-start | bytes 786440 | tf_op jit(solution)/shard_map/ppermute | solution.py:235
  110.2 5.0 %collective-permute-done.35.arrived = bf16[512,256]{1,0:T(8,128)(2,1)S(1)} collective-permute-done((bf16[512,256]{1,0:T(8,128)(2,1)S(1)}, bf16[512,256]{1,0:T(8,128)(2,1)S(1)}, u32[]{:S(2)}, u32[]{:S(2)}) %collective-permute-start.35) | collective-permute-done | bytes 262176 | tf_op jit(solution)/shard_map/ppermute | solution.py:236
  115.9 1.6 %collective-permute-start.26 = (bf16[512,256]{1,0:T(8,128)(2,1)S(1)}, bf16[512,256]{1,0:T(8,128)(2,1)S(1)}, u32[]{:S(2)}, u32[]{:S(2)}) collective-permute-start(bf16[512,256]{1,0:T(8,128)(2,1)S(1)} %add_convert_fusion.6), channel_id=1, source_target_pairs={{0,8},{8,16},{16,24},{24,28},{28,20},{20,12},{12,4},{4,0},{1,9},{9... | collective-permute-start | bytes 786440 | tf_op jit(solution)/shard_map/ppermute | solution.py:235
  117.5 7.1 %collective-permute-done.26.arrived = bf16[512,256]{1,0:T(8,128)(2,1)S(1)} collective-permute-done((bf16[512,256]{1,0:T(8,128)(2,1)S(1)}, bf16[512,256]{1,0:T(8,128)(2,1)S(1)}, u32[]{:S(2)}, u32[]{:S(2)}) %collective-permute-start.26) | collective-permute-done | bytes 262176 | tf_op jit(solution)/shard_map/ppermute | solution.py:235
  127.9 6.7 %collective-permute-done.37 = bf16[1,512,256]{2,1,0:T(8,128)(2,1)S(1)} collective-permute-done((bf16[1,512,256]{2,1,0:T(8,128)(2,1)S(1)}, bf16[1,512,256]{2,1,0:T(8,128)(2,1)S(1)}, u32[]{:S(2)}, u32[]{:S(2)}) %collective-permute-start.37) | collective-permute-done | bytes 262176 | tf_op jit(solution)/shard_map/ppermute | solution.py:190
  134.6 5.2 %collective-permute-done.28 = bf16[1,512,256]{2,1,0:T(8,128)(2,1)S(1)} collective-permute-done((bf16[1,512,256]{2,1,0:T(8,128)(2,1)S(1)}, bf16[1,512,256]{2,1,0:T(8,128)(2,1)S(1)}, u32[]{:S(2)}, u32[]{:S(2)}) %collective-permute-start.28) | collective-permute-done | bytes 262176 | tf_op jit(solution)/shard_map/ppermute | solution.py:190
  (114 shorter events, 21.6 us)
Async XLA Ops:
  0.0 12.9 %copy-start = (s32[64,128]{1,0:T(8,128)S(1)}, s32[64,128]{1,0:T(8,128)}, u32[]{:S(2)}) copy-start(s32[64,128]{1,0:T(8,128)} %param.15) | copy-start | bytes 98308
  0.0 28.1 %copy-start.2 = (bf16[1024,256]{1,0:T(8,128)(2,1)S(1)}, bf16[1024,256]{1,0:T(8,128)(2,1)}, u32[]{:S(2)}) copy-start(bf16[1024,256]{1,0:T(8,128)(2,1)} %refs_0_.3) | copy-start | bytes 1572868
  0.0 28.1 %copy-start.3 = (bf16[1024,512]{1,0:T(8,128)(2,1)S(1)}, bf16[1024,512]{1,0:T(8,128)(2,1)}, u32[]{:S(2)}) copy-start(bf16[1024,512]{1,0:T(8,128)(2,1)} %refs_4_.3) | copy-start | bytes 3145732
  0.0 23.7 %collective-permute-start.1 = (bf16[1024,256]{1,0:T(8,128)(2,1)}, bf16[1024,256]{1,0:T(8,128)(2,1)S(1)}, u32[]{:S(2)}, u32[]{:S(2)}) collective-permute-start(bf16[1024,256]{1,0:T(8,128)(2,1)} %refs_0_.3), channel_id=1, source_target_pairs={{0,2},{1,3},{2,0},{3,1},{4,6},{5,7},{6,4},{7,5},{8,10},{9,11},{10,... | collective-permute-start | bytes 1572872 | tf_op jit(solution)/shard_map/ppermute | solution.py:190
  3.0 25.0 %collective-permute-start = (bf16[1024,256]{1,0:T(8,128)(2,1)}, bf16[1024,256]{1,0:T(8,128)(2,1)S(1)}, u32[]{:S(2)}, u32[]{:S(2)}) collective-permute-start(bf16[1024,256]{1,0:T(8,128)(2,1)} %refs_0_.3), channel_id=1, source_target_pairs={{0,1},{1,0},{2,3},{3,2},{4,5},{5,4},{6,7},{7,6},{8,9},{9,8},{10,11... | collective-permute-start | bytes 1572872 | tf_op jit(solution)/shard_map/ppermute | solution.py:190
  5.3 9.6 %collective-permute-start.3 = (s32[1,1088]{1,0:T(1,128)S(1)}, s32[1,1088]{1,0:T(1,128)S(1)}, u32[]{:S(2)}, u32[]{:S(2)}) collective-permute-start(s32[1,1088]{1,0:T(1,128)S(1)} %broadcast_in_dim.54), channel_id=1, source_target_pairs={{0,4},{4,0},{8,12},{12,8},{16,20},{20,16},{24,28},{28,24},{1,5},{5... | collective-permute-start | bytes 13064 | tf_op jit(solution)/shard_map/ppermute | solution.py:190
  14.9 3.7 %collective-permute-start.4 = (s32[2,1088]{1,0:T(2,128)S(1)}, s32[2,1088]{1,0:T(2,128)S(1)}, u32[]{:S(2)}, u32[]{:S(2)}) collective-permute-start(s32[2,1088]{1,0:T(2,128)S(1)} %pad_add_fusion.2), channel_id=1, source_target_pairs={{0,8},{4,12},{8,0},{12,4},{16,24},{20,28},{24,16},{28,20},{1,9},{5... | collective-permute-start | bytes 26120 | tf_op jit(solution)/shard_map/ppermute | solution.py:190
  18.7 4.7 %collective-permute-start.5 = (s32[4,1088]{1,0:T(4,128)S(1)}, s32[4,1088]{1,0:T(4,128)S(1)}, u32[]{:S(2)}, u32[]{:S(2)}) collective-permute-start(s32[4,1088]{1,0:T(4,128)S(1)} %pad_add_fusion.1), channel_id=1, source_target_pairs={{0,16},{4,20},{8,24},{12,28},{16,0},{20,4},{24,8},{28,12},{1,17},{... | collective-permute-start | bytes 52232 | tf_op jit(solution)/shard_map/ppermute | solution.py:190
  23.7 7.8 %copy-start.1 = (bf16[64,128,512]{2,1,0:T(8,128)(2,1)S(1)}, bf16[64,128,512]{2,1,0:T(8,128)(2,1)}, u32[]{:S(2)}) copy-start(bf16[64,128,512]{2,1,0:T(8,128)(2,1)} %cache.15) | copy-start | bytes 25165828
  23.7 4.4 %collective-permute-start.2 = (bf16[1024,256]{1,0:T(8,128)(2,1)S(1)}, bf16[1024,256]{1,0:T(8,128)(2,1)S(1)}, u32[]{:S(2)}, u32[]{:S(2)}) collective-permute-start(bf16[1024,256]{1,0:T(8,128)(2,1)S(1)} %collective-permute-done.1.refs_2_), channel_id=1, source_target_pairs={{0,1},{1,0},{2,3},{3,2},{4,5},{5,4},{6,7},{7,6},{8,9},{9,8},{10,11... | collective-permute-start | bytes 1572872 | tf_op jit(solution)/shard_map/ppermute | solution.py:190
  29.4 8.7 %collective-permute-start.13 = (bf16[512,256]{1,0:T(8,128)(2,1)S(1)}, bf16[512,256]{1,0:T(8,128)(2,1)S(1)}, u32[]{:S(2)}, u32[]{:S(2)}) collective-permute-start(bf16[512,256]{1,0:T(8,128)(2,1)S(1)} %get-tuple-element.55.q_b), channel_id=1, source_target_pairs={{8,0},{16,8},{24,16},{28,24},{20,28},{12,20},{4,12},{0,4},{9,1},{1... | collective-permute-start | bytes 786440 | tf_op jit(solution)/shard_map/ppermute | solution.py:230
  30.0 8.7 %collective-permute-start.6 = (bf16[512,256]{1,0:T(8,128)(2,1)S(1)}, bf16[512,256]{1,0:T(8,128)(2,1)S(1)}, u32[]{:S(2)}, u32[]{:S(2)}) collective-permute-start(bf16[512,256]{1,0:T(8,128)(2,1)S(1)} %get-tuple-element.56.q_a), channel_id=1, source_target_pairs={{0,8},{8,16},{16,24},{24,28},{28,20},{20,12},{12,4},{4,0},{1,9},{9... | collective-permute-start | bytes 786440 | tf_op jit(solution)/shard_map/ppermute | solution.py:229
  38.2 8.7 %collective-permute-start.14 = (bf16[512,256]{1,0:T(8,128)(2,1)S(1)}, bf16[512,256]{1,0:T(8,128)(2,1)S(1)}, u32[]{:S(2)}, u32[]{:S(2)}) collective-permute-start(bf16[512,256]{1,0:T(8,128)(2,1)S(1)} %collective-permute-done.13.q_b), channel_id=1, source_target_pairs={{8,0},{16,8},{24,16},{28,24},{20,28},{12,20},{4,12},{0,4},{9,1},{1... | collective-permute-start | bytes 786440 | tf_op jit(solution)/shard_map/ppermute | solution.py:230
  38.7 8.7 %collective-permute-start.7 = (bf16[512,256]{1,0:T(8,128)(2,1)S(1)}, bf16[512,256]{1,0:T(8,128)(2,1)S(1)}, u32[]{:S(2)}, u32[]{:S(2)}) collective-permute-start(bf16[512,256]{1,0:T(8,128)(2,1)S(1)} %collective-permute-done.6.q_a), channel_id=1, source_target_pairs={{0,8},{8,16},{16,24},{24,28},{28,20},{20,12},{12,4},{4,0},{1,9},{9... | collective-permute-start | bytes 786440 | tf_op jit(solution)/shard_map/ppermute | solution.py:229
  43.4 9.3 %collective-permute-start.29 = (bf16[512,256]{1,0:T(8,128)(2,1)S(1)}, bf16[512,256]{1,0:T(8,128)(2,1)S(1)}, u32[]{:S(2)}, u32[]{:S(2)}) collective-permute-start(bf16[512,256]{1,0:T(8,128)(2,1)S(1)} %convert_element_type.130), channel_id=1, source_target_pairs={{8,0},{16,8},{24,16},{28,24},{20,28},{12,20},{4,12},{0,4},{9,1},{1... | collective-permute-start | bytes 786440 | tf_op jit(solution)/shard_map/ppermute | solution.py:236
  46.8 11.6 %collective-permute-start.15 = (bf16[512,256]{1,0:T(8,128)(2,1)S(1)}, bf16[512,256]{1,0:T(8,128)(2,1)S(1)}, u32[]{:S(2)}, u32[]{:S(2)}) collective-permute-start(bf16[512,256]{1,0:T(8,128)(2,1)S(1)} %collective-permute-done.14.q_b), channel_id=1, source_target_pairs={{8,0},{16,8},{24,16},{28,24},{20,28},{12,20},{4,12},{0,4},{9,1},{1... | collective-permute-start | bytes 786440 | tf_op jit(solution)/shard_map/ppermute | solution.py:230
  47.3 11.6 %collective-permute-start.8 = (bf16[512,256]{1,0:T(8,128)(2,1)S(1)}, bf16[512,256]{1,0:T(8,128)(2,1)S(1)}, u32[]{:S(2)}, u32[]{:S(2)}) collective-permute-start(bf16[512,256]{1,0:T(8,128)(2,1)S(1)} %collective-permute-done.7.q_a), channel_id=1, source_target_pairs={{0,8},{8,16},{16,24},{24,28},{28,20},{20,12},{12,4},{4,0},{1,9},{9... | collective-permute-start | bytes 786440 | tf_op jit(solution)/shard_map/ppermute | solution.py:229
  52.8 11.2 %collective-permute-start.30 = (bf16[512,256]{1,0:T(8,128)(2,1)S(1)}, bf16[512,256]{1,0:T(8,128)(2,1)S(1)}, u32[]{:S(2)}, u32[]{:S(2)}) collective-permute-start(bf16[512,256]{1,0:T(8,128)(2,1)S(1)} %add_convert_fusion.5), channel_id=1, source_target_pairs={{8,0},{16,8},{24,16},{28,24},{20,28},{12,20},{4,12},{0,4},{9,1},{1... | collective-permute-start | bytes 786440 | tf_op jit(solution)/shard_map/ppermute | solution.py:236
  54.7 9.9 %collective-permute-start.20 = (bf16[512,256]{1,0:T(8,128)(2,1)S(1)}, bf16[512,256]{1,0:T(8,128)(2,1)S(1)}, u32[]{:S(2)}, u32[]{:S(2)}) collective-permute-start(bf16[512,256]{1,0:T(8,128)(2,1)S(1)} %convert_element_type.113), channel_id=1, source_target_pairs={{0,8},{8,16},{16,24},{24,28},{28,20},{20,12},{12,4},{4,0},{1,9},{9... | collective-permute-start | bytes 786440 | tf_op jit(solution)/shard_map/ppermute | solution.py:235
  58.4 11.2 %collective-permute-start.16 = (bf16[512,256]{1,0:T(8,128)(2,1)S(1)}, bf16[512,256]{1,0:T(8,128)(2,1)S(1)}, u32[]{:S(2)}, u32[]{:S(2)}) collective-permute-start(bf16[512,256]{1,0:T(8,128)(2,1)S(1)} %collective-permute-done.15.q_b), channel_id=1, source_target_pairs={{8,0},{16,8},{24,16},{28,24},{20,28},{12,20},{4,12},{0,4},{9,1},{1... | collective-permute-start | bytes 786440 | tf_op jit(solution)/shard_map/ppermute | solution.py:230
  58.9 11.2 %collective-permute-start.9 = (bf16[512,256]{1,0:T(8,128)(2,1)S(1)}, bf16[512,256]{1,0:T(8,128)(2,1)S(1)}, u32[]{:S(2)}, u32[]{:S(2)}) collective-permute-start(bf16[512,256]{1,0:T(8,128)(2,1)S(1)} %collective-permute-done.8.q_a), channel_id=1, source_target_pairs={{0,8},{8,16},{16,24},{24,28},{28,20},{20,12},{12,4},{4,0},{1,9},{9... | collective-permute-start | bytes 786440 | tf_op jit(solution)/shard_map/ppermute | solution.py:229
  64.0 11.2 %collective-permute-start.31 = (bf16[512,256]{1,0:T(8,128)(2,1)S(1)}, bf16[512,256]{1,0:T(8,128)(2,1)S(1)}, u32[]{:S(2)}, u32[]{:S(2)}) collective-permute-start(bf16[512,256]{1,0:T(8,128)(2,1)S(1)} %add_convert_fusion.4), channel_id=1, source_target_pairs={{8,0},{16,8},{24,16},{28,24},{20,28},{12,20},{4,12},{0,4},{9,1},{1... | collective-permute-start | bytes 786440 | tf_op jit(solution)/shard_map/ppermute | solution.py:236
  64.7 11.2 %collective-permute-start.21 = (bf16[512,256]{1,0:T(8,128)(2,1)S(1)}, bf16[512,256]{1,0:T(8,128)(2,1)S(1)}, u32[]{:S(2)}, u32[]{:S(2)}) collective-permute-start(bf16[512,256]{1,0:T(8,128)(2,1)S(1)} %add_convert_fusion.11), channel_id=1, source_target_pairs={{0,8},{8,16},{16,24},{24,28},{28,20},{20,12},{12,4},{4,0},{1,9},{9... | collective-permute-start | bytes 786440 | tf_op jit(solution)/shard_map/ppermute | solution.py:235
  69.6 11.2 %collective-permute-start.17 = (bf16[512,256]{1,0:T(8,128)(2,1)S(1)}, bf16[512,256]{1,0:T(8,128)(2,1)S(1)}, u32[]{:S(2)}, u32[]{:S(2)}) collective-permute-start(bf16[512,256]{1,0:T(8,128)(2,1)S(1)} %collective-permute-done.16.q_b), channel_id=1, source_target_pairs={{8,0},{16,8},{24,16},{28,24},{20,28},{12,20},{4,12},{0,4},{9,1},{1... | collective-permute-start | bytes 786440 | tf_op jit(solution)/shard_map/ppermute | solution.py:230
  70.1 11.2 %collective-permute-start.10 = (bf16[512,256]{1,0:T(8,128)(2,1)S(1)}, bf16[512,256]{1,0:T(8,128)(2,1)S(1)}, u32[]{:S(2)}, u32[]{:S(2)}) collective-permute-start(bf16[512,256]{1,0:T(8,128)(2,1)S(1)} %collective-permute-done.9.q_a), channel_id=1, source_target_pairs={{0,8},{8,16},{16,24},{24,28},{28,20},{20,12},{12,4},{4,0},{1,9},{9... | collective-permute-start | bytes 786440 | tf_op jit(solution)/shard_map/ppermute | solution.py:229
  75.3 11.2 %collective-permute-start.32 = (bf16[512,256]{1,0:T(8,128)(2,1)S(1)}, bf16[512,256]{1,0:T(8,128)(2,1)S(1)}, u32[]{:S(2)}, u32[]{:S(2)}) collective-permute-start(bf16[512,256]{1,0:T(8,128)(2,1)S(1)} %add_convert_fusion.3), channel_id=1, source_target_pairs={{8,0},{16,8},{24,16},{28,24},{20,28},{12,20},{4,12},{0,4},{9,1},{1... | collective-permute-start | bytes 786440 | tf_op jit(solution)/shard_map/ppermute | solution.py:236
  75.9 11.2 %collective-permute-start.22 = (bf16[512,256]{1,0:T(8,128)(2,1)S(1)}, bf16[512,256]{1,0:T(8,128)(2,1)S(1)}, u32[]{:S(2)}, u32[]{:S(2)}) collective-permute-start(bf16[512,256]{1,0:T(8,128)(2,1)S(1)} %add_convert_fusion.10), channel_id=1, source_target_pairs={{0,8},{8,16},{16,24},{24,28},{28,20},{20,12},{12,4},{4,0},{1,9},{9... | collective-permute-start | bytes 786440 | tf_op jit(solution)/shard_map/ppermute | solution.py:235
  80.8 11.2 %collective-permute-start.18 = (bf16[512,256]{1,0:T(8,128)(2,1)S(1)}, bf16[512,256]{1,0:T(8,128)(2,1)S(1)}, u32[]{:S(2)}, u32[]{:S(2)}) collective-permute-start(bf16[512,256]{1,0:T(8,128)(2,1)S(1)} %collective-permute-done.17.q_b), channel_id=1, source_target_pairs={{8,0},{16,8},{24,16},{28,24},{20,28},{12,20},{4,12},{0,4},{9,1},{1... | collective-permute-start | bytes 786440 | tf_op jit(solution)/shard_map/ppermute | solution.py:230
  81.4 11.2 %collective-permute-start.11 = (bf16[512,256]{1,0:T(8,128)(2,1)S(1)}, bf16[512,256]{1,0:T(8,128)(2,1)S(1)}, u32[]{:S(2)}, u32[]{:S(2)}) collective-permute-start(bf16[512,256]{1,0:T(8,128)(2,1)S(1)} %collective-permute-done.10.q_a), channel_id=1, source_target_pairs={{0,8},{8,16},{16,24},{24,28},{28,20},{20,12},{12,4},{4,0},{1,9},{9... | collective-permute-start | bytes 786440 | tf_op jit(solution)/shard_map/ppermute | solution.py:229
  86.5 11.2 %collective-permute-start.33 = (bf16[512,256]{1,0:T(8,128)(2,1)S(1)}, bf16[512,256]{1,0:T(8,128)(2,1)S(1)}, u32[]{:S(2)}, u32[]{:S(2)}) collective-permute-start(bf16[512,256]{1,0:T(8,128)(2,1)S(1)} %add_convert_fusion.2), channel_id=1, source_target_pairs={{8,0},{16,8},{24,16},{28,24},{20,28},{12,20},{4,12},{0,4},{9,1},{1... | collective-permute-start | bytes 786440 | tf_op jit(solution)/shard_map/ppermute | solution.py:236
  87.2 11.4 %collective-permute-start.23 = (bf16[512,256]{1,0:T(8,128)(2,1)S(1)}, bf16[512,256]{1,0:T(8,128)(2,1)S(1)}, u32[]{:S(2)}, u32[]{:S(2)}) collective-permute-start(bf16[512,256]{1,0:T(8,128)(2,1)S(1)} %add_convert_fusion.9), channel_id=1, source_target_pairs={{0,8},{8,16},{16,24},{24,28},{28,20},{20,12},{12,4},{4,0},{1,9},{9... | collective-permute-start | bytes 786440 | tf_op jit(solution)/shard_map/ppermute | solution.py:235
  92.1 11.2 %collective-permute-start.19 = (bf16[512,256]{1,0:T(8,128)(2,1)S(1)}, bf16[512,256]{1,0:T(8,128)(2,1)S(1)}, u32[]{:S(2)}, u32[]{:S(2)}) collective-permute-start(bf16[512,256]{1,0:T(8,128)(2,1)S(1)} %collective-permute-done.18.q_b), channel_id=1, source_target_pairs={{8,0},{16,8},{24,16},{28,24},{20,28},{12,20},{4,12},{0,4},{9,1},{1... | collective-permute-start | bytes 786440 | tf_op jit(solution)/shard_map/ppermute | solution.py:230
  92.6 10.7 %collective-permute-start.12 = (bf16[512,256]{1,0:T(8,128)(2,1)S(1)}, bf16[512,256]{1,0:T(8,128)(2,1)S(1)}, u32[]{:S(2)}, u32[]{:S(2)}) collective-permute-start(bf16[512,256]{1,0:T(8,128)(2,1)S(1)} %collective-permute-done.11.q_a), channel_id=1, source_target_pairs={{0,8},{8,16},{16,24},{24,28},{28,20},{20,12},{12,4},{4,0},{1,9},{9... | collective-permute-start | bytes 786440 | tf_op jit(solution)/shard_map/ppermute | solution.py:229
  97.7 10.1 %collective-permute-start.34 = (bf16[512,256]{1,0:T(8,128)(2,1)S(1)}, bf16[512,256]{1,0:T(8,128)(2,1)S(1)}, u32[]{:S(2)}, u32[]{:S(2)}) collective-permute-start(bf16[512,256]{1,0:T(8,128)(2,1)S(1)} %add_convert_fusion.1), channel_id=1, source_target_pairs={{8,0},{16,8},{24,16},{28,24},{20,28},{12,20},{4,12},{0,4},{9,1},{1... | collective-permute-start | bytes 786440 | tf_op jit(solution)/shard_map/ppermute | solution.py:236
  98.6 9.9 %collective-permute-start.24 = (bf16[512,256]{1,0:T(8,128)(2,1)S(1)}, bf16[512,256]{1,0:T(8,128)(2,1)S(1)}, u32[]{:S(2)}, u32[]{:S(2)}) collective-permute-start(bf16[512,256]{1,0:T(8,128)(2,1)S(1)} %add_convert_fusion.8), channel_id=1, source_target_pairs={{0,8},{8,16},{16,24},{24,28},{28,20},{20,12},{12,4},{4,0},{1,9},{9... | collective-permute-start | bytes 786440 | tf_op jit(solution)/shard_map/ppermute | solution.py:235
  103.3 11.9 %copy-start.4 = (bf16[256,1024]{1,0:T(8,128)(2,1)S(1)}, bf16[256,1024]{1,0:T(8,128)(2,1)}, u32[]{:S(2)}) copy-start(bf16[256,1024]{1,0:T(8,128)(2,1)} %w_out.3) | copy-start | bytes 1572868
  107.9 7.3 %collective-permute-start.35 = (bf16[512,256]{1,0:T(8,128)(2,1)S(1)}, bf16[512,256]{1,0:T(8,128)(2,1)S(1)}, u32[]{:S(2)}, u32[]{:S(2)}) collective-permute-start(bf16[512,256]{1,0:T(8,128)(2,1)S(1)} %add_convert_fusion), channel_id=1, source_target_pairs={{8,0},{16,8},{24,16},{28,24},{20,28},{12,20},{4,12},{0,4},{9,1},{1... | collective-permute-start | bytes 786440 | tf_op jit(solution)/shard_map/ppermute | solution.py:236
  108.6 7.2 %collective-permute-start.25 = (bf16[512,256]{1,0:T(8,128)(2,1)S(1)}, bf16[512,256]{1,0:T(8,128)(2,1)S(1)}, u32[]{:S(2)}, u32[]{:S(2)}) collective-permute-start(bf16[512,256]{1,0:T(8,128)(2,1)S(1)} %add_convert_fusion.7), channel_id=1, source_target_pairs={{0,8},{8,16},{16,24},{24,28},{28,20},{20,12},{12,4},{4,0},{1,9},{9... | collective-permute-start | bytes 786440 | tf_op jit(solution)/shard_map/ppermute | solution.py:235
  115.7 9.5 %collective-permute-start.36 = (bf16[2,512,256]{2,1,0:T(8,128)(2,1)S(1)}, bf16[2,512,256]{2,1,0:T(8,128)(2,1)S(1)}, u32[]{:S(2)}, u32[]{:S(2)}) collective-permute-start(bf16[2,512,256]{2,1,0:T(8,128)(2,1)S(1)} %get-tuple-element.50), channel_id=1, source_target_pairs={{0,1},{1,0},{2,3},{3,2},{4,5},{5,4},{6,7},{7,6},{8,9},{9,8},{10,11... | collective-permute-start | bytes 1572872 | tf_op jit(solution)/shard_map/ppermute | solution.py:190
  115.9 8.7 %collective-permute-start.26 = (bf16[512,256]{1,0:T(8,128)(2,1)S(1)}, bf16[512,256]{1,0:T(8,128)(2,1)S(1)}, u32[]{:S(2)}, u32[]{:S(2)}) collective-permute-start(bf16[512,256]{1,0:T(8,128)(2,1)S(1)} %add_convert_fusion.6), channel_id=1, source_target_pairs={{0,8},{8,16},{16,24},{24,28},{28,20},{20,12},{12,4},{4,0},{1,9},{9... | collective-permute-start | bytes 786440 | tf_op jit(solution)/shard_map/ppermute | solution.py:235
  125.2 2.0 %collective-permute-start.27 = (bf16[2,512,256]{2,1,0:T(8,128)(2,1)S(1)}, bf16[2,512,256]{2,1,0:T(8,128)(2,1)S(1)}, u32[]{:S(2)}, u32[]{:S(2)}) collective-permute-start(bf16[2,512,256]{2,1,0:T(8,128)(2,1)S(1)} %get-tuple-element.40), channel_id=1, source_target_pairs={{0,1},{1,0},{2,3},{3,2},{4,5},{5,4},{6,7},{7,6},{8,9},{9,8},{10,11... | collective-permute-start | bytes 1572872 | tf_op jit(solution)/shard_map/ppermute | solution.py:190
  125.4 9.2 %collective-permute-start.37 = (bf16[1,512,256]{2,1,0:T(8,128)(2,1)S(1)}, bf16[1,512,256]{2,1,0:T(8,128)(2,1)S(1)}, u32[]{:S(2)}, u32[]{:S(2)}) collective-permute-start(bf16[1,512,256]{2,1,0:T(8,128)(2,1)S(1)} %slice.131), channel_id=1, source_target_pairs={{0,2},{1,3},{2,0},{3,1},{4,6},{5,7},{6,4},{7,5},{8,10},{9,11},{10,... | collective-permute-start | bytes 786440 | tf_op jit(solution)/shard_map/ppermute | solution.py:190
  127.3 12.5 %collective-permute-start.28 = (bf16[1,512,256]{2,1,0:T(8,128)(2,1)S(1)}, bf16[1,512,256]{2,1,0:T(8,128)(2,1)S(1)}, u32[]{:S(2)}, u32[]{:S(2)}) collective-permute-start(bf16[1,512,256]{2,1,0:T(8,128)(2,1)S(1)} %slice.132), channel_id=1, source_target_pairs={{0,2},{1,3},{2,0},{3,1},{4,6},{5,7},{6,4},{7,5},{8,10},{9,11},{10,... | collective-permute-start | bytes 786440 | tf_op jit(solution)/shard_map/ppermute | solution.py:190
where the time goes:
time: 141 us
  waiting for transfers between devices  54.1 us (38%)
  starting transfers between devices  39.8 us (28%)
  Pallas kernels  29.3 us (21%)
  other arithmetic  9.47 us (7%)
  local copies, waits for them, and re-layouts  7.65 us (5%)
    pallas_call x8, Pallas kernels, attend(): pl.pallas_call(functools.partial(attend_kernel, heads, cap), out_shape=(o...  25.8 us
    ppermute x7, waiting for transfers between devices, per_device(): q_b = lax.ppermute(q_b, 'user', back)  21.3 us
    ppermute x10, waiting for transfers between devices, swap(): lax.ppermute(value, axis, [(i, i ^ bit) for i in range(lax.axis_size(axis...  17.1 us
    ppermute x7, starting transfers between devices, per_device(): sum_a = lax.ppermute(term_a.astype(jnp.bfloat16), 'user', onward)  11.1 us
    ppermute x7, starting transfers between devices, per_device(): q_a = lax.ppermute(q_a, 'user', onward)  10.4 us
    ppermute x10, starting transfers between devices, swap(): lax.ppermute(value, axis, [(i, i ^ bit) for i in range(lax.axis_size(axis...  10.2 us
    ppermute x7, waiting for transfers between devices, per_device(): sum_b = lax.ppermute(term_b.astype(jnp.bfloat16), 'user', back)  8.46 us
    ppermute x7, waiting for transfers between devices, per_device(): sum_a = lax.ppermute(term_a.astype(jnp.bfloat16), 'user', onward)  7.13 us
  transfers between devices with their start and end apart: 38, of which 20 were waited for; matrix products, arithmetic and copies ran while one was open for 11% of the time, Pallas kernels for 20%

commit v1 on v0

v1 whole, which is shorter than its diff:
```python
import functools

import jax
import jax.numpy as jnp
import numpy as np
from jax import lax
from jax.experimental import pallas as pl
from jax.experimental.pallas import tpu as pltpu
from jax.sharding import PartitionSpec as P

DH = 128
EVENTS = 128
norm_eps = 1e-06
MASKED = -1e30
FACT_ROWS = 16

VMEM = pl.BlockSpec(memory_space=pltpu.VMEM)
SMEM = pl.BlockSpec(memory_space=pltpu.SMEM)


def pin(value):
    return pltpu.with_memory_space_constraint(value, pltpu.VMEM)


def in_hbm(value):
    return pltpu.with_memory_space_constraint(value, pltpu.HBM)


def ring_order(count):
    wide = 1
    while 4 * wide * wide <= count:
        wide *= 2
    deep = count // wide
    order = [z * wide for z in range(deep)]
    for turn, z in enumerate(reversed(range(deep))):
        across = range(1, wide) if turn % 2 == 0 else reversed(range(1, wide))
        order += [z * wide + x for x in across]
    return order


def owner_users(block_count, block_table, slot_count):
    user_count, most_blocks = block_table.shape
    live_mask = jnp.arange(most_blocks, dtype=jnp.int32)[None, :] < block_count[:, None]
    slot_hit = (
        block_table[:, :, None] == jnp.arange(slot_count, dtype=jnp.int32)[None, None, :]
    ) & live_mask[:, :, None]
    user_label = jnp.arange(user_count, dtype=jnp.int32)[:, None, None] + 1
    return jnp.sum(jnp.where(slot_hit, user_label, 0), axis=(0, 1)) - 1


def silu(value):
    return value * (0.5 + 0.5 * jnp.tanh(0.5 * value))


def near_kernel(first, second, mate, w_in, cache, partial, w_here, cache_here, sems):
    copies = [
        pltpu.make_async_copy(source, target, sems.at[i])
        for i, (source, target) in enumerate(((w_in, w_here), (cache, cache_here)))
    ]
    for copy in copies:
        copy.start()
    copies[0].wait()
    half, width = first.shape
    part = lax.axis_index("tp")
    own, other = (
        w_here[pl.ds(pl.multiple_of((part ^ m) * width, width), width)] for m in range(2)
    )
    for begin, piece in ((0, first), (half, second)):
        rows = slice(begin, begin + half)
        partial[rows] = jnp.dot(
            piece[...], own, preferred_element_type=jnp.float32
        ) + jnp.dot(mate[rows], other, preferred_element_type=jnp.float32)
    copies[1].wait()


def near(first, second, mate, w_in, cache):
    rows, width = mate.shape
    hbm = pl.BlockSpec(memory_space=pltpu.HBM)
    held = [jax.ShapeDtypeStruct(value.shape, value.dtype) for value in (w_in, cache)]
    return pl.pallas_call(
        near_kernel,
        out_shape=(jax.ShapeDtypeStruct((rows, w_in.shape[1]), jnp.float32), *held),
        in_specs=[VMEM] * 3 + [hbm] * 2,
        out_specs=(VMEM,) * 3,
        scratch_shapes=[pltpu.SemaphoreType.DMA((2,))],
        compiler_params=pltpu.CompilerParams(vmem_limit_bytes=8 * 1024 * 1024),
        cost_estimate=pl.CostEstimate(
            flops=4 * rows * width * w_in.shape[1],
            bytes_accessed=4 * rows * w_in.shape[1] + 2 * cache.size,
            transcendentals=0,
        ),
        name="near",
    )(pin(first), pin(second), pin(mate), in_hbm(w_in), in_hbm(cache))


def project_kernel(heads, gate, begin, first, partial, *refs):
    slices, (w_in, facts, out) = refs[:-3], refs[-3:]
    rows, width = slices[0].shape
    part = lax.axis_index("tp")
    for h in range(heads):
        column = (2 * h + gate) * DH
        total = partial[begin : begin + rows, column : column + DH]
        for m, piece in enumerate(slices):
            start = pl.multiple_of((part ^ (m + first)) * width, width)
            total += jnp.dot(
                piece[...],
                w_in[pl.ds(start, width), column : column + DH],
                preferred_element_type=jnp.float32,
            )
        out[:rows, h * DH : (h + 1) * DH] = silu(total).astype(jnp.bfloat16)
    if not gate:
        out[rows:] = facts[...]


def project(partial, slices, w_in, facts, heads, gate, begin, first):
    rows = slices[0].shape[0]
    return pl.pallas_call(
        functools.partial(project_kernel, heads, gate, begin, first),
        out_shape=jax.ShapeDtypeStruct(
            (rows + (0 if gate else FACT_ROWS), heads * DH), jnp.bfloat16
        ),
        in_specs=[VMEM] * (len(slices) + 3),
        out_specs=VMEM,
        compiler_params=pltpu.CompilerParams(vmem_limit_bytes=8 * 1024 * 1024),
        name="gates" if gate else "queries",
    )(pin(partial), *[pin(piece) for piece in slices], pin(w_in), pin(facts))


def attend_kernel(heads, cap, step, begin, route, slots, event_mask, q, cache, out):
    rows, width = out.shape
    me = lax.axis_index("user")
    index = route[me, step]
    labels = lax.broadcasted_iota(jnp.int32, (DH, EVENTS), 0)

    facts = q[rows:].astype(jnp.float32).astype(jnp.int32)
    hot = []
    for row in range(begin, begin + rows, EVENTS):
        line, at = divmod(row, width)
        user = facts[line : line + 1, at : at + EVENTS]
        hot.append(jnp.where(user == labels, 1.0, 0.0).T.astype(jnp.bfloat16))
    hot = jnp.concatenate(hot, axis=0)

    line = 2 * rows // width
    owners = facts[line : line + 1, :DH]
    lanes = lax.broadcasted_iota(jnp.int32, (1, DH), 1)
    penalty = []
    for c in range(cap):
        owner = jnp.sum(jnp.where(lanes == me * cap + c, owners, 0), axis=1, keepdims=True)
        live = event_mask[pl.ds(slots[index, c], 1)] > 0
        label = jnp.where(live, owner, -1)
        penalty.append(jnp.where(label == labels, 0.0, MASKED).T.astype(jnp.bfloat16))

    per = min(2, cap)
    for h in range(heads):
        left = jnp.concatenate([q[:rows, h * DH : (h + 1) * DH], hot], axis=1)
        total = None
        for c in range(0, cap, per):
            held = [cache.at[slots[index, c + i]] for i in range(per)]
            keys = jnp.concatenate([b[:, 2 * h * DH : (2 * h + 1) * DH] for b in held], axis=0)
            values = jnp.concatenate(
                [b[:, (2 * h + 1) * DH : (2 * h + 2) * DH] for b in held], axis=0
            )
            right = jnp.concatenate([keys, jnp.concatenate(penalty[c : c + per], axis=0)], axis=1)
            half = lax.dot_general(
                left, right, (((1,), (1,)), ((), ())), preferred_element_type=jnp.float32
            ) * (0.5 * DH ** (-0.5))
            weights = (half + half * jnp.tanh(half)).astype(jnp.bfloat16)
            term = jnp.dot(weights, values, preferred_element_type=jnp.float32)
            total = term if total is None else total + term
        out[:, h * DH : (h + 1) * DH] = total


def attend(step, begin, route, slots, event_mask, q, cache, heads, cap):
    rows = q.shape[0] - FACT_ROWS
    return pl.pallas_call(
        functools.partial(attend_kernel, heads, cap, step, begin),
        out_shape=jax.ShapeDtypeStruct((rows, heads * DH), jnp.float32),
        in_specs=[SMEM] * 2 + [VMEM] * 3,
        out_specs=VMEM,
        compiler_params=pltpu.CompilerParams(vmem_limit_bytes=8 * 1024 * 1024),
        name="attend",
    )(route, slots, pin(event_mask), pin(q), pin(cache))


def finish_kernel(heads, parts, own, arrived, gates, w_out, sent, kept):
    part = lax.axis_index("tp")
    columns = []
    for h in range(heads):
        at = slice(h * DH, (h + 1) * DH)
        value = own[:, at] + arrived[:, at].astype(jnp.float32)
        scale = lax.rsqrt(jnp.mean(value * value, axis=1, keepdims=True) + norm_eps)
        columns.append((value * scale * gates[:, at].astype(jnp.float32)).astype(jnp.bfloat16))
    hidden = jnp.concatenate(columns, axis=1)
    width = w_out.shape[1] // parts
    for m in range(parts):
        start = pl.multiple_of((part ^ m) * width, width)
        term = jnp.dot(hidden, w_out[:, pl.ds(start, width)], preferred_element_type=jnp.float32)
        if m % 2:
            sent[m // 2] = term.astype(jnp.bfloat16)
        else:
            kept[m // 2] = term


def finish(own, arrived, gates, w_out, heads, parts):
    rows = own.shape[0]
    width = w_out.shape[1] // parts
    return pl.pallas_call(
        functools.partial(finish_kernel, heads, parts),
        out_shape=(
            jax.ShapeDtypeStruct((parts // 2, rows, width), jnp.bfloat16),
            jax.ShapeDtypeStruct((parts // 2, rows, width), jnp.float32),
        ),
        in_specs=[VMEM] * 4,
        out_specs=(VMEM, VMEM),
        compiler_params=pltpu.CompilerParams(vmem_limit_bytes=8 * 1024 * 1024),
        name="finish",
    )(pin(own), pin(arrived), pin(gates), pin(w_out))


def per_device(
    cand_feats, w_in, w_out, kv_cache, event_mask, block_counts, user_blocks, send_slots, cand_user
):
    row_count, slice_width = cand_feats.shape
    heads = w_out.shape[0] // DH
    peers = lax.axis_size("user")
    parts = lax.axis_size("tp")
    cap = send_slots.shape[1]
    half = row_count // 2

    order = ring_order(peers)
    route = np.zeros((peers, peers), np.int32)
    for position, index in enumerate(order):
        route[index] = [order[(position - step) % peers] for step in range(peers)]
    route = jnp.array(route)
    onward = [(order[i], order[(i + 1) % peers]) for i in range(peers)]
    back = [(b, a) for a, b in onward]

    def swap(value, axis, bit):
        return lax.ppermute(value, axis, [(i, i ^ bit) for i in range(lax.axis_size(axis))])

    def bits(count):
        return [1 << b for b in range(count.bit_length() - 1)]

    begins = (half, 0)
    width = heads * DH
    slot_users = owner_users(block_counts, user_blocks, peers * cap)
    users = cand_user.reshape(-1, width)
    owners = jnp.pad(slot_users, (0, width - peers * cap))[None]
    facts = jnp.concatenate([users, owners], axis=0).astype(jnp.bfloat16)
    facts = jnp.pad(facts, ((0, FACT_ROWS - facts.shape[0]), (0, 0)))

    rows = {begin: cand_feats[begin : begin + half] for begin in begins}
    mate, facts = lax.optimization_barrier((swap(cand_feats, "tp", 1), facts))
    partial, w_in, cache = near(rows[0], rows[half], mate, w_in, kv_cache)
    queries, gates = {}, {}
    last = partial
    for begin in begins:
        far = {0: rows[begin]}
        if begin != begins[0]:
            far, _ = lax.optimization_barrier((far, partial))
        for bit in reversed(bits(parts)[1:]):
            far.update({m | bit: swap(value, "tp", bit) for m, value in far.items()})
        del far[0]
        far, last = lax.optimization_barrier((far, last))
        far.update({m | 1: swap(value, "tp", 1) for m, value in far.items()})
        far = [far[m] for m in range(2, parts)]
        queries[begin] = project(partial, far, w_in, facts, heads, 0, begin, 2)
        gates[begin] = project(partial, far, w_in, facts, heads, 1, begin, 2)
        last = queries[begin]

    def score(step, begin, query):
        return attend(step, begin, route, send_slots, event_mask, query, cache, heads, cap)

    way = {0: onward, half: back}
    queries_at = {begin: [queries[begin]] for begin in begins}
    for begin in begins:
        for step in range(1, peers):
            queries_at[begin].append(lax.ppermute(queries_at[begin][-1], "user", way[begin]))
    own, sums = {}, {}
    last = None
    turns = [(step, begin) for step in range(1, peers) for begin in begins]
    turns[5:5] = [(0, half)]
    turns[8:8] = [(0, 0)]
    for step, begin in turns:
        query = queries_at[begin][step]
        if last is not None:
            query, last = lax.optimization_barrier((query, last))
        last = term = score(step if begin == 0 else (peers - step) % peers, begin, query)
        if step == 0:
            own[begin] = term
            continue
        if begin in sums:
            term = term + sums[begin].astype(jnp.float32)
        sums[begin] = lax.ppermute(term.astype(jnp.bfloat16), "user", way[begin])

    scored = {}
    for begin in begins:
        sent, kept = finish(own[begin], sums[begin], gates[begin], w_out, heads, parts)
        for bit in bits(parts):
            total = kept + swap(sent, "tp", bit).astype(jnp.float32)
            sent, kept = total[1::2].astype(jnp.bfloat16), total[::2]
        scored[begin] = (rows[begin].astype(jnp.float32) + total[0]).astype(jnp.bfloat16)
    return jnp.concatenate([scored[0], scored[half]], axis=0)


def solution(mesh):
    in_specs = (
        P("user", "tp"),
        P(None, "tp"),
        P("tp", None),
        P("user", None, "tp"),
        P("user", None),
        P("user"),
        P("user", None),
        P("user", None),
        P("user"),
    )
    out_specs = P("user", "tp")
    return jax.shard_map(
        per_device, mesh=mesh, in_specs=in_specs, out_specs=out_specs, check_vma=False
    )
```

time: 141 us -> 130 us (0.922)
  waiting for transfers between devices: 54.1 us -> 37.9 us
  Pallas kernels: 29.3 us -> 44.6 us
  local copies, waits for them, and re-layouts: 7.65 us -> 1.18 us
  other arithmetic: 9.47 us -> 4.3 us
  starting transfers between devices: 39.8 us -> 41.8 us
    ppermute x28, waiting for transfers between devices: 37 us -> 19.8 us  [the longest x14 9.99 us: per_device(): lax.ppermute(queries_at[begin][-1], 'user', way[begin])]
    pallas_call x10 -> x21, Pallas kernels: 28.3 us -> 43.5 us  [the longest x16 38 us: attend(): pl.pallas_call(functools.partial(attend_kernel, heads, cap, step, begin),...]
    gather x5 -> x0, local copies, waits for them, and re-layouts: 5.69 us -> none  [the longest x1 1.3 us: per_device(): sequence[(here + steps) % peers]]
    convert_element_type x17 -> x15, other arithmetic: 5.27 us -> 1.01 us  [the longest x14 0.82 us: per_device(): sums[begin] = lax.ppermute(term.astype(jnp.bfloat16), 'user', way[begin])]
    ppermute x28, starting transfers between devices: 29.6 us -> 33.3 us  [the longest x14 16.8 us: per_device(): lax.ppermute(queries_at[begin][-1], 'user', way[begin])]
    ppermute x10 -> x9, starting transfers between devices: 10.2 us -> 8.45 us  [swap(): lax.ppermute(value, axis, [(i, i ^ bit) for i in range(lax.axis_size(axis...]
    ppermute x10 -> x9, waiting for transfers between devices: 17.1 us -> 18.1 us  [swap(): lax.ppermute(value, axis, [(i, i ^ bit) for i in range(lax.axis_size(axis...]
  transfers between devices with their start and end apart: 38 -> 37, of which waited for: 20 -> 15; matrix products, arithmetic and copies ran while one was open for 11% -> 3% of each run, Pallas kernels for 20% -> 34%
where the time goes in v1:
time: 130 us
  Pallas kernels  44.6 us (34%)
  starting transfers between devices  41.8 us (32%)
  waiting for transfers between devices  37.9 us (29%)
  other arithmetic  4.3 us (3%)
    pallas_call x16, Pallas kernels, attend(): pl.pallas_call(functools.partial(attend_kernel, heads, cap, step, begin),...  38 us
    ppermute x9, waiting for transfers between devices, swap(): lax.ppermute(value, axis, [(i, i ^ bit) for i in range(lax.axis_size(axis...  18.1 us
    ppermute x14, starting transfers between devices, per_device(): lax.ppermute(queries_at[begin][-1], 'user', way[begin])  16.8 us
    ppermute x14, starting transfers between devices, per_device(): sums[begin] = lax.ppermute(term.astype(jnp.bfloat16), 'user', way[begin])  16.5 us
    ppermute x14, waiting for transfers between devices, per_device(): lax.ppermute(queries_at[begin][-1], 'user', way[begin])  9.99 us
    ppermute x14, waiting for transfers between devices, per_device(): sums[begin] = lax.ppermute(term.astype(jnp.bfloat16), 'user', way[begin])  9.78 us
    ppermute x9, starting transfers between devices, swap(): lax.ppermute(value, axis, [(i, i ^ bit) for i in range(lax.axis_size(axis...  8.45 us
    pallas_call x1, Pallas kernels, near(): pl.pallas_call(near_kernel, out_shape=(jax.ShapeDtypeStruct((rows, w_in.s...  3.75 us
  transfers between devices with their start and end apart: 37, of which 15 were waited for; matrix products, arithmetic and copies ran while one was open for 3% of the time, Pallas kernels for 34%

profile of v1, /device:TPU:0, one launch (start us, length us, event | category | flops | bytes accessed | tf_op | source)
XLA Modules:
  0.0 130.1 jit_solution(16803346314893173029)
XLA Ops:
  1.5 2.6 %collective-permute-start.2 = (bf16[512,256]{1,0:T(8,128)(2,1)S(1)}, bf16[512,256]{1,0:T(8,128)(2,1)S(1)}, u32[]{:S(2)}, u32[]{:S(2)}) collective-permute-start(bf16[512,256]{1,0:T(8,128)(2,1)S(1)} %get-tuple-element.61.second), channel_id=1, source_target_pairs={{0,2},{1,3},{2,0},{3,1},{4,6},{5,7},{6,4},{7,5},{8,10},{9,11},{10,... | collective-permute-start | bytes 786440 | tf_op jit(solution)/shard_map/ppermute | solution.py:239
  6.4 3.7 %near.1 = (f32[1024,512]{1,0:T(8,128)S(1)}, bf16[1024,512]{1,0:T(8,128)(2,1)S(1)}, bf16[64,128,512]{2,1,0:T(8,128)(2,1)S(1)}) custom-call(bf16[512,256]{1,0:T(8,128)(2,1)S(1)} %get-tuple-element.34.first, bf16[512,256]{1,0:T(8,128)(2,1)S(1)} %get-tuple-element.61.second, bf16[1024,256]{1,0:T(8,128)(2,1)S(1)} %collective-permute-done.mate, ...), custom_call_target="tpu_custom_call" | custom-call | flops 536870912 | bytes 10485760 | tf_op jit(solution)/shard_map/near/pallas_call | solution.py:80
  11.1 1.7 %collective-permute-start.1 = (bf16[512,256]{1,0:T(8,128)(2,1)S(1)}, bf16[512,256]{1,0:T(8,128)(2,1)S(1)}, u32[]{:S(2)}, u32[]{:S(2)}) collective-permute-start(bf16[512,256]{1,0:T(8,128)(2,1)S(1)} %get-tuple-element.34.first), channel_id=1, source_target_pairs={{0,2},{1,3},{2,0},{3,1},{4,6},{5,7},{6,4},{7,5},{8,10},{9,11},{10,... | collective-permute-start | bytes 786440 | tf_op jit(solution)/shard_map/ppermute | solution.py:239
  13.3 1.6 %collective-permute-start.5 = (bf16[528,256]{1,0:T(8,128)(2,1)S(1)}, bf16[528,256]{1,0:T(8,128)(2,1)S(1)}, u32[]{:S(2)}, u32[]{:S(2)}) collective-permute-start(bf16[528,256]{1,0:T(8,128)(2,1)S(1)} %queries.2.q), channel_id=1, source_target_pairs={{8,0},{16,8},{24,16},{28,24},{20,28},{12,20},{4,12},{0,4},{9,1},{1... | collective-permute-start | bytes 811016 | tf_op jit(solution)/shard_map/ppermute | solution.py:278
  14.8 5.0 %collective-permute-done.1.refs_0_ = bf16[512,256]{1,0:T(8,128)(2,1)S(1)} collective-permute-done((bf16[512,256]{1,0:T(8,128)(2,1)S(1)}, bf16[512,256]{1,0:T(8,128)(2,1)S(1)}, u32[]{:S(2)}, u32[]{:S(2)}) %collective-permute-start.1) | collective-permute-done | bytes 262176 | tf_op jit(solution)/shard_map/ppermute | solution.py:239
  19.8 1.5 %collective-permute-done.4.refs_1_ = bf16[512,256]{1,0:T(8,128)(2,1)S(1)} collective-permute-done((bf16[512,256]{1,0:T(8,128)(2,1)S(1)}, bf16[512,256]{1,0:T(8,128)(2,1)S(1)}, u32[]{:S(2)}, u32[]{:S(2)}) %collective-permute-start.4) | collective-permute-done | bytes 262176 | tf_op jit(solution)/shard_map/ppermute | solution.py:239
  21.8 1.8 %collective-permute-start.9 = (bf16[528,256]{1,0:T(8,128)(2,1)S(1)}, bf16[528,256]{1,0:T(8,128)(2,1)S(1)}, u32[]{:S(2)}, u32[]{:S(2)}) collective-permute-start(bf16[528,256]{1,0:T(8,128)(2,1)S(1)} %queries.3.q), channel_id=1, source_target_pairs={{0,8},{8,16},{16,24},{24,28},{28,20},{20,12},{12,4},{4,0},{1,9},{9... | collective-permute-start | bytes 811016 | tf_op jit(solution)/shard_map/ppermute | solution.py:278
  23.9 2.4 %attend.16 = f32[512,256]{1,0:T(8,128)S(1)} custom-call(s32[8,8]{1,0:T(8,128)S(1)} %copy-done.3, s32[8,8]{1,0:T(8,128)S(1)} %copy-done.2, s32[64,128]{1,0:T(8,128)S(1)} %copy-done, bf16[528,256]{1,0:T(8,128)(2,1)S(1)} %collective-permute-done.5.q, bf16[64,128,512]{2,1,0:T(8,128)(2,1)S(1)} %get-tuple-element.39.cache), custom_call_target="tpu_custom_call" | custom-call | tf_op jit(solution)/shard_map/attend/pallas_call | solution.py:175
  26.3 1.8 %collective-permute-start.28 = (bf16[512,256]{1,0:T(8,128)(2,1)S(1)}, bf16[512,256]{1,0:T(8,128)(2,1)S(1)}, u32[]{:S(2)}, u32[]{:S(2)}) collective-permute-start(bf16[512,256]{1,0:T(8,128)(2,1)S(1)} %convert_element_type.125), channel_id=1, source_target_pairs={{8,0},{16,8},{24,16},{28,24},{20,28},{12,20},{4,12},{0,4},{9,1},{1... | collective-permute-start | bytes 786440 | tf_op jit(solution)/shard_map/ppermute | solution.py:294
  28.1 2.3 %collective-permute-done.9.q = bf16[528,256]{1,0:T(8,128)(2,1)S(1)} collective-permute-done((bf16[528,256]{1,0:T(8,128)(2,1)S(1)}, bf16[528,256]{1,0:T(8,128)(2,1)S(1)}, u32[]{:S(2)}, u32[]{:S(2)}) %collective-permute-start.9) | collective-permute-done | bytes 270368 | tf_op jit(solution)/shard_map/ppermute | solution.py:278
  30.4 2.4 %attend.17 = f32[512,256]{1,0:T(8,128)S(1)} custom-call(s32[8,8]{1,0:T(8,128)S(1)} %copy-done.3, s32[8,8]{1,0:T(8,128)S(1)} %copy-done.2, s32[64,128]{1,0:T(8,128)S(1)} %copy-done, bf16[528,256]{1,0:T(8,128)(2,1)S(1)} %collective-permute-done.9.q, bf16[64,128,512]{2,1,0:T(8,128)(2,1)S(1)} %get-tuple-element.39.cache), custom_call_target="tpu_custom_call" | custom-call | tf_op jit(solution)/shard_map/attend/pallas_call | solution.py:175
  32.7 1.8 %collective-permute-start.10 = (bf16[528,256]{1,0:T(8,128)(2,1)S(1)}, bf16[528,256]{1,0:T(8,128)(2,1)S(1)}, u32[]{:S(2)}, u32[]{:S(2)}) collective-permute-start(bf16[528,256]{1,0:T(8,128)(2,1)S(1)} %collective-permute-done.9.q), channel_id=1, source_target_pairs={{0,8},{8,16},{16,24},{24,28},{28,20},{20,12},{12,4},{4,0},{1,9},{9... | collective-permute-start | bytes 811016 | tf_op jit(solution)/shard_map/ppermute | solution.py:278
  34.6 2.4 %attend.18 = f32[512,256]{1,0:T(8,128)S(1)} custom-call(s32[8,8]{1,0:T(8,128)S(1)} %copy-done.3, s32[8,8]{1,0:T(8,128)S(1)} %copy-done.2, s32[64,128]{1,0:T(8,128)S(1)} %copy-done, bf16[528,256]{1,0:T(8,128)(2,1)S(1)} %collective-permute-done.6.q, bf16[64,128,512]{2,1,0:T(8,128)(2,1)S(1)} %get-tuple-element.39.cache), custom_call_target="tpu_custom_call" | custom-call | tf_op jit(solution)/shard_map/attend/pallas_call | solution.py:175
  37.6 1.5 %collective-permute-start.29 = (bf16[512,256]{1,0:T(8,128)(2,1)S(1)}, bf16[512,256]{1,0:T(8,128)(2,1)S(1)}, u32[]{:S(2)}, u32[]{:S(2)}) collective-permute-start(bf16[512,256]{1,0:T(8,128)(2,1)S(1)} %add_convert_fusion.5), channel_id=1, source_target_pairs={{8,0},{16,8},{24,16},{28,24},{20,28},{12,20},{4,12},{0,4},{9,1},{1... | collective-permute-start | bytes 786440 | tf_op jit(solution)/shard_map/ppermute | solution.py:294
  39.7 1.3 collective-permute-done.10.q
  41.0 2.4 %attend.19 = f32[512,256]{1,0:T(8,128)S(1)} custom-call(s32[8,8]{1,0:T(8,128)S(1)} %copy-done.3, s32[8,8]{1,0:T(8,128)S(1)} %copy-done.2, s32[64,128]{1,0:T(8,128)S(1)} %copy-done, bf16[528,256]{1,0:T(8,128)(2,1)S(1)} %collective-permute-done.10.q, bf16[64,128,512]{2,1,0:T(8,128)(2,1)S(1)} %get-tuple-element.39.cache), custom_call_target="tpu_custom_call" | custom-call | tf_op jit(solution)/shard_map/attend/pallas_call | solution.py:175
  43.4 2.5 %collective-permute-start.11 = (bf16[528,256]{1,0:T(8,128)(2,1)S(1)}, bf16[528,256]{1,0:T(8,128)(2,1)S(1)}, u32[]{:S(2)}, u32[]{:S(2)}) collective-permute-start(bf16[528,256]{1,0:T(8,128)(2,1)S(1)} %collective-permute-done.10.q), channel_id=1, source_target_pairs={{0,8},{8,16},{16,24},{24,28},{28,20},{20,12},{12,4},{4,0},{1,9},{9... | collective-permute-start | bytes 811016 | tf_op jit(solution)/shard_map/ppermute | solution.py:278
  46.4 2.4 %attend.20 = f32[512,256]{1,0:T(8,128)S(1)} custom-call(s32[8,8]{1,0:T(8,128)S(1)} %copy-done.3, s32[8,8]{1,0:T(8,128)S(1)} %copy-done.2, s32[64,128]{1,0:T(8,128)S(1)} %copy-done, bf16[528,256]{1,0:T(8,128)(2,1)S(1)} %collective-permute-done.7.q, bf16[64,128,512]{2,1,0:T(8,128)(2,1)S(1)} %get-tuple-element.39.cache), custom_call_target="tpu_custom_call" | custom-call | tf_op jit(solution)/shard_map/attend/pallas_call | solution.py:175
  49.1 3.0 %collective-permute-done.29 = bf16[512,256]{1,0:T(8,128)(2,1)S(1)} collective-permute-done((bf16[512,256]{1,0:T(8,128)(2,1)S(1)}, bf16[512,256]{1,0:T(8,128)(2,1)S(1)}, u32[]{:S(2)}, u32[]{:S(2)}) %collective-permute-start.29) | collective-permute-done | bytes 262176 | tf_op jit(solution)/shard_map/ppermute | solution.py:294
  52.5 2.0 %collective-permute-start.20 = (bf16[512,256]{1,0:T(8,128)(2,1)S(1)}, bf16[512,256]{1,0:T(8,128)(2,1)S(1)}, u32[]{:S(2)}, u32[]{:S(2)}) collective-permute-start(bf16[512,256]{1,0:T(8,128)(2,1)S(1)} %add_convert_fusion.11), channel_id=1, source_target_pairs={{0,8},{8,16},{16,24},{24,28},{28,20},{20,12},{12,4},{4,0},{1,9},{9... | collective-permute-start | bytes 786440 | tf_op jit(solution)/shard_map/ppermute | solution.py:294
  54.5 2.4 %attend.21.own = f32[512,256]{1,0:T(8,128)S(1)} custom-call(s32[8,8]{1,0:T(8,128)S(1)} %copy-done.3, s32[8,8]{1,0:T(8,128)S(1)} %copy-done.2, s32[64,128]{1,0:T(8,128)S(1)} %copy-done, bf16[528,256]{1,0:T(8,128)(2,1)S(1)} %queries.2.q, bf16[64,128,512]{2,1,0:T(8,128)(2,1)S(1)} %get-tuple-element.39.cache), custom_call_target="tpu_custom_call" | custom-call | tf_op jit(solution)/shard_map/attend/pallas_call | solution.py:175
  56.9 2.4 %attend.22 = f32[512,256]{1,0:T(8,128)S(1)} custom-call(s32[8,8]{1,0:T(8,128)S(1)} %copy-done.3, s32[8,8]{1,0:T(8,128)S(1)} %copy-done.2, s32[64,128]{1,0:T(8,128)S(1)} %copy-done, bf16[528,256]{1,0:T(8,128)(2,1)S(1)} %collective-permute-done.11.q, bf16[64,128,512]{2,1,0:T(8,128)(2,1)S(1)} %get-tuple-element.39.cache), custom_call_target="tpu_custom_call" | custom-call | tf_op jit(solution)/shard_map/attend/pallas_call | solution.py:175
  59.3 1.6 %collective-permute-start.12 = (bf16[528,256]{1,0:T(8,128)(2,1)S(1)}, bf16[528,256]{1,0:T(8,128)(2,1)S(1)}, u32[]{:S(2)}, u32[]{:S(2)}) collective-permute-start(bf16[528,256]{1,0:T(8,128)(2,1)S(1)} %collective-permute-done.11.q), channel_id=1, source_target_pairs={{0,8},{8,16},{16,24},{24,28},{28,20},{20,12},{12,4},{4,0},{1,9},{9... | collective-permute-start | bytes 811016 | tf_op jit(solution)/shard_map/ppermute | solution.py:278
  60.9 2.4 %attend.23 = f32[512,256]{1,0:T(8,128)S(1)} custom-call(s32[8,8]{1,0:T(8,128)S(1)} %copy-done.3, s32[8,8]{1,0:T(8,128)S(1)} %copy-done.2, s32[64,128]{1,0:T(8,128)S(1)} %copy-done, bf16[528,256]{1,0:T(8,128)(2,1)S(1)} %collective-permute-done.8.q, bf16[64,128,512]{2,1,0:T(8,128)(2,1)S(1)} %get-tuple-element.39.cache), custom_call_target="tpu_custom_call" | custom-call | tf_op jit(solution)/shard_map/attend/pallas_call | solution.py:175
  64.2 1.8 %collective-permute-start.21 = (bf16[512,256]{1,0:T(8,128)(2,1)S(1)}, bf16[512,256]{1,0:T(8,128)(2,1)S(1)}, u32[]{:S(2)}, u32[]{:S(2)}) collective-permute-start(bf16[512,256]{1,0:T(8,128)(2,1)S(1)} %add_convert_fusion.10), channel_id=1, source_target_pairs={{0,8},{8,16},{16,24},{24,28},{28,20},{20,12},{12,4},{4,0},{1,9},{9... | collective-permute-start | bytes 786440 | tf_op jit(solution)/shard_map/ppermute | solution.py:294
  66.1 2.4 %attend.24.own = f32[512,256]{1,0:T(8,128)S(1)} custom-call(s32[8,8]{1,0:T(8,128)S(1)} %copy-done.3, s32[8,8]{1,0:T(8,128)S(1)} %copy-done.2, s32[64,128]{1,0:T(8,128)S(1)} %copy-done, bf16[528,256]{1,0:T(8,128)(2,1)S(1)} %queries.3.q, bf16[64,128,512]{2,1,0:T(8,128)(2,1)S(1)} %get-tuple-element.39.cache), custom_call_target="tpu_custom_call" | custom-call | tf_op jit(solution)/shard_map/attend/pallas_call | solution.py:175
  68.5 2.4 %attend.25 = f32[512,256]{1,0:T(8,128)S(1)} custom-call(s32[8,8]{1,0:T(8,128)S(1)} %copy-done.3, s32[8,8]{1,0:T(8,128)S(1)} %copy-done.2, s32[64,128]{1,0:T(8,128)S(1)} %copy-done, bf16[528,256]{1,0:T(8,128)(2,1)S(1)} %collective-permute-done.12.q, bf16[64,128,512]{2,1,0:T(8,128)(2,1)S(1)} %get-tuple-element.39.cache), custom_call_target="tpu_custom_call" | custom-call | tf_op jit(solution)/shard_map/attend/pallas_call | solution.py:175
  70.8 1.6 %collective-permute-start.13 = (bf16[528,256]{1,0:T(8,128)(2,1)S(1)}, bf16[528,256]{1,0:T(8,128)(2,1)S(1)}, u32[]{:S(2)}, u32[]{:S(2)}) collective-permute-start(bf16[528,256]{1,0:T(8,128)(2,1)S(1)} %collective-permute-done.12.q), channel_id=1, source_target_pairs={{0,8},{8,16},{16,24},{24,28},{28,20},{20,12},{12,4},{4,0},{1,9},{9... | collective-permute-start | bytes 811016 | tf_op jit(solution)/shard_map/ppermute | solution.py:278
  72.5 2.4 %attend.26 = f32[512,256]{1,0:T(8,128)S(1)} custom-call(s32[8,8]{1,0:T(8,128)S(1)} %copy-done.3, s32[8,8]{1,0:T(8,128)S(1)} %copy-done.2, s32[64,128]{1,0:T(8,128)S(1)} %copy-done, bf16[528,256]{1,0:T(8,128)(2,1)S(1)} %collective-permute-done.16.q, bf16[64,128,512]{2,1,0:T(8,128)(2,1)S(1)} %get-tuple-element.39.cache), custom_call_target="tpu_custom_call" | custom-call | tf_op jit(solution)/shard_map/attend/pallas_call | solution.py:175
  76.2 1.4 %collective-permute-start.22 = (bf16[512,256]{1,0:T(8,128)(2,1)S(1)}, bf16[512,256]{1,0:T(8,128)(2,1)S(1)}, u32[]{:S(2)}, u32[]{:S(2)}) collective-permute-start(bf16[512,256]{1,0:T(8,128)(2,1)S(1)} %add_convert_fusion.9), channel_id=1, source_target_pairs={{0,8},{8,16},{16,24},{24,28},{28,20},{20,12},{12,4},{4,0},{1,9},{9... | collective-permute-start | bytes 786440 | tf_op jit(solution)/shard_map/ppermute | solution.py:294
  77.6 1.9 %collective-permute-done.13.q = bf16[528,256]{1,0:T(8,128)(2,1)S(1)} collective-permute-done((bf16[528,256]{1,0:T(8,128)(2,1)S(1)}, bf16[528,256]{1,0:T(8,128)(2,1)S(1)}, u32[]{:S(2)}, u32[]{:S(2)}) %collective-permute-start.13) | collective-permute-done | bytes 270368 | tf_op jit(solution)/shard_map/ppermute | solution.py:278
  79.5 2.4 %attend.27 = f32[512,256]{1,0:T(8,128)S(1)} custom-call(s32[8,8]{1,0:T(8,128)S(1)} %copy-done.3, s32[8,8]{1,0:T(8,128)S(1)} %copy-done.2, s32[64,128]{1,0:T(8,128)S(1)} %copy-done, bf16[528,256]{1,0:T(8,128)(2,1)S(1)} %collective-permute-done.13.q, bf16[64,128,512]{2,1,0:T(8,128)(2,1)S(1)} %get-tuple-element.39.cache), custom_call_target="tpu_custom_call" | custom-call | tf_op jit(solution)/shard_map/attend/pallas_call | solution.py:175
  81.9 2.1 %collective-permute-start.14 = (bf16[528,256]{1,0:T(8,128)(2,1)S(1)}, bf16[528,256]{1,0:T(8,128)(2,1)S(1)}, u32[]{:S(2)}, u32[]{:S(2)}) collective-permute-start(bf16[528,256]{1,0:T(8,128)(2,1)S(1)} %collective-permute-done.13.q), channel_id=1, source_target_pairs={{0,8},{8,16},{16,24},{24,28},{28,20},{20,12},{12,4},{4,0},{1,9},{9... | collective-permute-start | bytes 811016 | tf_op jit(solution)/shard_map/ppermute | solution.py:278
  84.0 2.4 %attend.28 = f32[512,256]{1,0:T(8,128)S(1)} custom-call(s32[8,8]{1,0:T(8,128)S(1)} %copy-done.3, s32[8,8]{1,0:T(8,128)S(1)} %copy-done.2, s32[64,128]{1,0:T(8,128)S(1)} %copy-done, bf16[528,256]{1,0:T(8,128)(2,1)S(1)} %collective-permute-done.17.q, bf16[64,128,512]{2,1,0:T(8,128)(2,1)S(1)} %get-tuple-element.39.cache), custom_call_target="tpu_custom_call" | custom-call | tf_op jit(solution)/shard_map/attend/pallas_call | solution.py:175
  86.7 1.6 %collective-permute-start.33 = (bf16[512,256]{1,0:T(8,128)(2,1)S(1)}, bf16[512,256]{1,0:T(8,128)(2,1)S(1)}, u32[]{:S(2)}, u32[]{:S(2)}) collective-permute-start(bf16[512,256]{1,0:T(8,128)(2,1)S(1)} %add_convert_fusion.1), channel_id=1, source_target_pairs={{8,0},{16,8},{24,16},{28,24},{20,28},{12,20},{4,12},{0,4},{9,1},{1... | collective-permute-start | bytes 786440 | tf_op jit(solution)/shard_map/ppermute | solution.py:294
  88.9 2.7 %collective-permute-done.14.q = bf16[528,256]{1,0:T(8,128)(2,1)S(1)} collective-permute-done((bf16[528,256]{1,0:T(8,128)(2,1)S(1)}, bf16[528,256]{1,0:T(8,128)(2,1)S(1)}, u32[]{:S(2)}, u32[]{:S(2)}) %collective-permute-start.14) | collective-permute-done | bytes 270368 | tf_op jit(solution)/shard_map/ppermute | solution.py:278
  91.6 2.4 %attend.29 = f32[512,256]{1,0:T(8,128)S(1)} custom-call(s32[8,8]{1,0:T(8,128)S(1)} %copy-done.3, s32[8,8]{1,0:T(8,128)S(1)} %copy-done.2, s32[64,128]{1,0:T(8,128)S(1)} %copy-done, bf16[528,256]{1,0:T(8,128)(2,1)S(1)} %collective-permute-done.14.q, bf16[64,128,512]{2,1,0:T(8,128)(2,1)S(1)} %get-tuple-element.39.cache), custom_call_target="tpu_custom_call" | custom-call | tf_op jit(solution)/shard_map/attend/pallas_call | solution.py:175
  94.0 1.6 %collective-permute-start.15 = (bf16[528,256]{1,0:T(8,128)(2,1)S(1)}, bf16[528,256]{1,0:T(8,128)(2,1)S(1)}, u32[]{:S(2)}, u32[]{:S(2)}) collective-permute-start(bf16[528,256]{1,0:T(8,128)(2,1)S(1)} %collective-permute-done.14.q), channel_id=1, source_target_pairs={{0,8},{8,16},{16,24},{24,28},{28,20},{20,12},{12,4},{4,0},{1,9},{9... | collective-permute-start | bytes 811016 | tf_op jit(solution)/shard_map/ppermute | solution.py:278
  95.6 2.4 %attend.30 = f32[512,256]{1,0:T(8,128)S(1)} custom-call(s32[8,8]{1,0:T(8,128)S(1)} %copy-done.3, s32[8,8]{1,0:T(8,128)S(1)} %copy-done.2, s32[64,128]{1,0:T(8,128)S(1)} %copy-done, bf16[528,256]{1,0:T(8,128)(2,1)S(1)} %collective-permute-done.18.q, bf16[64,128,512]{2,1,0:T(8,128)(2,1)S(1)} %get-tuple-element.39.cache), custom_call_target="tpu_custom_call" | custom-call | tf_op jit(solution)/shard_map/attend/pallas_call | solution.py:175
  98.7 1.6 %collective-permute-start.24 = (bf16[512,256]{1,0:T(8,128)(2,1)S(1)}, bf16[512,256]{1,0:T(8,128)(2,1)S(1)}, u32[]{:S(2)}, u32[]{:S(2)}) collective-permute-start(bf16[512,256]{1,0:T(8,128)(2,1)S(1)} %add_convert_fusion.7), channel_id=1, source_target_pairs={{0,8},{8,16},{16,24},{24,28},{28,20},{20,12},{12,4},{4,0},{1,9},{9... | collective-permute-start | bytes 786440 | tf_op jit(solution)/shard_map/ppermute | solution.py:294
  100.7 1.3 %collective-permute-done.15.q = bf16[528,256]{1,0:T(8,128)(2,1)S(1)} collective-permute-done((bf16[528,256]{1,0:T(8,128)(2,1)S(1)}, bf16[528,256]{1,0:T(8,128)(2,1)S(1)}, u32[]{:S(2)}, u32[]{:S(2)}) %collective-permute-start.15) | collective-permute-done | bytes 270368 | tf_op jit(solution)/shard_map/ppermute | solution.py:278
  102.1 2.4 %attend.31 = f32[512,256]{1,0:T(8,128)S(1)} custom-call(s32[8,8]{1,0:T(8,128)S(1)} %copy-done.3, s32[8,8]{1,0:T(8,128)S(1)} %copy-done.2, s32[64,128]{1,0:T(8,128)S(1)} %copy-done, bf16[528,256]{1,0:T(8,128)(2,1)S(1)} %collective-permute-done.15.q, bf16[64,128,512]{2,1,0:T(8,128)(2,1)S(1)} %get-tuple-element.39.cache), custom_call_target="tpu_custom_call" | custom-call | tf_op jit(solution)/shard_map/attend/pallas_call | solution.py:175
  105.2 1.8 %collective-permute-start.25 = (bf16[512,256]{1,0:T(8,128)(2,1)S(1)}, bf16[512,256]{1,0:T(8,128)(2,1)S(1)}, u32[]{:S(2)}, u32[]{:S(2)}) collective-permute-start(bf16[512,256]{1,0:T(8,128)(2,1)S(1)} %add_convert_fusion.6), channel_id=1, source_target_pairs={{0,8},{8,16},{16,24},{24,28},{28,20},{20,12},{12,4},{4,0},{1,9},{9... | collective-permute-start | bytes 786440 | tf_op jit(solution)/shard_map/ppermute | solution.py:294
  107.5 6.5 %collective-permute-done.25.arrived = bf16[512,256]{1,0:T(8,128)(2,1)S(1)} collective-permute-done((bf16[512,256]{1,0:T(8,128)(2,1)S(1)}, bf16[512,256]{1,0:T(8,128)(2,1)S(1)}, u32[]{:S(2)}, u32[]{:S(2)}) %collective-permute-start.25) | collective-permute-done | bytes 262176 | tf_op jit(solution)/shard_map/ppermute | solution.py:294
  114.7 1.8 %collective-permute-start.36 = (bf16[1,512,256]{2,1,0:T(8,128)(2,1)S(1)}, bf16[1,512,256]{2,1,0:T(8,128)(2,1)S(1)}, u32[]{:S(2)}, u32[]{:S(2)}) collective-permute-start(bf16[1,512,256]{2,1,0:T(8,128)(2,1)S(1)} %slice.52), channel_id=1, source_target_pairs={{0,2},{1,3},{2,0},{3,1},{4,6},{5,7},{6,4},{7,5},{8,10},{9,11},{10,... | collective-permute-start | bytes 786440 | tf_op jit(solution)/shard_map/ppermute | solution.py:239
  116.7 1.7 %collective-permute-start.27 = (bf16[1,512,256]{2,1,0:T(8,128)(2,1)S(1)}, bf16[1,512,256]{2,1,0:T(8,128)(2,1)S(1)}, u32[]{:S(2)}, u32[]{:S(2)}) collective-permute-start(bf16[1,512,256]{2,1,0:T(8,128)(2,1)S(1)} %slice.53), channel_id=1, source_target_pairs={{0,2},{1,3},{2,0},{3,1},{4,6},{5,7},{6,4},{7,5},{8,10},{9,11},{10,... | collective-permute-start | bytes 786440 | tf_op jit(solution)/shard_map/ppermute | solution.py:239
  118.4 5.5 %collective-permute-done.36 = bf16[1,512,256]{2,1,0:T(8,128)(2,1)S(1)} collective-permute-done((bf16[1,512,256]{2,1,0:T(8,128)(2,1)S(1)}, bf16[1,512,256]{2,1,0:T(8,128)(2,1)S(1)}, u32[]{:S(2)}, u32[]{:S(2)}) %collective-permute-start.36) | collective-permute-done | bytes 262176 | tf_op jit(solution)/shard_map/ppermute | solution.py:239
  123.9 5.2 %collective-permute-done.27 = bf16[1,512,256]{2,1,0:T(8,128)(2,1)S(1)} collective-permute-done((bf16[1,512,256]{2,1,0:T(8,128)(2,1)S(1)}, bf16[1,512,256]{2,1,0:T(8,128)(2,1)S(1)}, u32[]{:S(2)}, u32[]{:S(2)}) %collective-permute-start.27) | collective-permute-done | bytes 262176 | tf_op jit(solution)/shard_map/ppermute | solution.py:239
  (89 shorter events, 15.7 us)
Async XLA Ops:
  0.0 6.4 %collective-permute-start = (bf16[1024,256]{1,0:T(8,128)(2,1)}, bf16[1024,256]{1,0:T(8,128)(2,1)S(1)}, u32[]{:S(2)}, u32[]{:S(2)}) collective-permute-start(bf16[1024,256]{1,0:T(8,128)(2,1)} %param.10), channel_id=1, source_target_pairs={{0,1},{1,0},{2,3},{3,2},{4,5},{5,4},{6,7},{7,6},{8,9},{9,8},{10,11... | collective-permute-start | bytes 1572872 | tf_op jit(solution)/shard_map/ppermute | solution.py:239
  1.5 9.6 %collective-permute-start.2 = (bf16[512,256]{1,0:T(8,128)(2,1)S(1)}, bf16[512,256]{1,0:T(8,128)(2,1)S(1)}, u32[]{:S(2)}, u32[]{:S(2)}) collective-permute-start(bf16[512,256]{1,0:T(8,128)(2,1)S(1)} %get-tuple-element.61.second), channel_id=1, source_target_pairs={{0,2},{1,3},{2,0},{3,1},{4,6},{5,7},{6,4},{7,5},{8,10},{9,11},{10,... | collective-permute-start | bytes 786440 | tf_op jit(solution)/shard_map/ppermute | solution.py:239
  6.4 17.5 %copy-start = (s32[64,128]{1,0:T(8,128)S(1)}, s32[64,128]{1,0:T(8,128)}, u32[]{:S(2)}) copy-start(s32[64,128]{1,0:T(8,128)} %event_mask.31) | copy-start | bytes 98308
  6.4 17.5 %copy-start.2 = (s32[8,8]{1,0:T(8,128)S(1)}, s32[8,8]{1,0:T(8,128)}, u32[]{:S(2)}) copy-start(s32[8,8]{1,0:T(8,128)} %slots.31) | copy-start | bytes 772
  6.4 17.5 %copy-start.3 = (s32[8,8]{1,0:T(8,128)S(1)}, s32[8,8]{1,0:T(8,128)}, u32[]{:S(2)}) copy-start(s32[8,8]{1,0:T(8,128)} %constant.12.clone.route) | copy-start | bytes 772
  11.1 1.7 %collective-permute-start.3 = (bf16[512,256]{1,0:T(8,128)(2,1)S(1)}, bf16[512,256]{1,0:T(8,128)(2,1)S(1)}, u32[]{:S(2)}, u32[]{:S(2)}) collective-permute-start(bf16[512,256]{1,0:T(8,128)(2,1)S(1)} %collective-permute-done.2.refs_0_), channel_id=1, source_target_pairs={{0,1},{1,0},{2,3},{3,2},{4,5},{5,4},{6,7},{7,6},{8,9},{9,8},{10,11... | collective-permute-start | bytes 786440 | tf_op jit(solution)/shard_map/ppermute | solution.py:239
  11.1 8.7 %collective-permute-start.1 = (bf16[512,256]{1,0:T(8,128)(2,1)S(1)}, bf16[512,256]{1,0:T(8,128)(2,1)S(1)}, u32[]{:S(2)}, u32[]{:S(2)}) collective-permute-start(bf16[512,256]{1,0:T(8,128)(2,1)S(1)} %get-tuple-element.34.first), channel_id=1, source_target_pairs={{0,2},{1,3},{2,0},{3,1},{4,6},{5,7},{6,4},{7,5},{8,10},{9,11},{10,... | collective-permute-start | bytes 786440 | tf_op jit(solution)/shard_map/ppermute | solution.py:239
  13.3 10.4 %collective-permute-start.5 = (bf16[528,256]{1,0:T(8,128)(2,1)S(1)}, bf16[528,256]{1,0:T(8,128)(2,1)S(1)}, u32[]{:S(2)}, u32[]{:S(2)}) collective-permute-start(bf16[528,256]{1,0:T(8,128)(2,1)S(1)} %queries.2.q), channel_id=1, source_target_pairs={{8,0},{16,8},{24,16},{28,24},{20,28},{12,20},{4,12},{0,4},{9,1},{1... | collective-permute-start | bytes 811016 | tf_op jit(solution)/shard_map/ppermute | solution.py:278
  19.8 1.5 %collective-permute-start.4 = (bf16[512,256]{1,0:T(8,128)(2,1)S(1)}, bf16[512,256]{1,0:T(8,128)(2,1)S(1)}, u32[]{:S(2)}, u32[]{:S(2)}) collective-permute-start(bf16[512,256]{1,0:T(8,128)(2,1)S(1)} %collective-permute-done.1.refs_0_), channel_id=1, source_target_pairs={{0,1},{1,0},{2,3},{3,2},{4,5},{5,4},{6,7},{7,6},{8,9},{9,8},{10,11... | collective-permute-start | bytes 786440 | tf_op jit(solution)/shard_map/ppermute | solution.py:239
  21.8 8.6 %collective-permute-start.9 = (bf16[528,256]{1,0:T(8,128)(2,1)S(1)}, bf16[528,256]{1,0:T(8,128)(2,1)S(1)}, u32[]{:S(2)}, u32[]{:S(2)}) collective-permute-start(bf16[528,256]{1,0:T(8,128)(2,1)S(1)} %queries.3.q), channel_id=1, source_target_pairs={{0,8},{8,16},{16,24},{24,28},{28,20},{20,12},{12,4},{4,0},{1,9},{9... | collective-permute-start | bytes 811016 | tf_op jit(solution)/shard_map/ppermute | solution.py:278
  23.6 11.0 %collective-permute-start.6 = (bf16[528,256]{1,0:T(8,128)(2,1)S(1)}, bf16[528,256]{1,0:T(8,128)(2,1)S(1)}, u32[]{:S(2)}, u32[]{:S(2)}) collective-permute-start(bf16[528,256]{1,0:T(8,128)(2,1)S(1)} %collective-permute-done.5.q), channel_id=1, source_target_pairs={{8,0},{16,8},{24,16},{28,24},{20,28},{12,20},{4,12},{0,4},{9,1},{1... | collective-permute-start | bytes 811016 | tf_op jit(solution)/shard_map/ppermute | solution.py:278
  26.3 11.2 %collective-permute-start.28 = (bf16[512,256]{1,0:T(8,128)(2,1)S(1)}, bf16[512,256]{1,0:T(8,128)(2,1)S(1)}, u32[]{:S(2)}, u32[]{:S(2)}) collective-permute-start(bf16[512,256]{1,0:T(8,128)(2,1)S(1)} %convert_element_type.125), channel_id=1, source_target_pairs={{8,0},{16,8},{24,16},{28,24},{20,28},{12,20},{4,12},{0,4},{9,1},{1... | collective-permute-start | bytes 786440 | tf_op jit(solution)/shard_map/ppermute | solution.py:294
  32.7 8.3 %collective-permute-start.10 = (bf16[528,256]{1,0:T(8,128)(2,1)S(1)}, bf16[528,256]{1,0:T(8,128)(2,1)S(1)}, u32[]{:S(2)}, u32[]{:S(2)}) collective-permute-start(bf16[528,256]{1,0:T(8,128)(2,1)S(1)} %collective-permute-done.9.q), channel_id=1, source_target_pairs={{0,8},{8,16},{16,24},{24,28},{28,20},{20,12},{12,4},{4,0},{1,9},{9... | collective-permute-start | bytes 811016 | tf_op jit(solution)/shard_map/ppermute | solution.py:278
  37.0 9.5 %collective-permute-start.7 = (bf16[528,256]{1,0:T(8,128)(2,1)S(1)}, bf16[528,256]{1,0:T(8,128)(2,1)S(1)}, u32[]{:S(2)}, u32[]{:S(2)}) collective-permute-start(bf16[528,256]{1,0:T(8,128)(2,1)S(1)} %collective-permute-done.6.q), channel_id=1, source_target_pairs={{8,0},{16,8},{24,16},{28,24},{20,28},{12,20},{4,12},{0,4},{9,1},{1... | collective-permute-start | bytes 811016 | tf_op jit(solution)/shard_map/ppermute | solution.py:278
  37.6 14.5 %collective-permute-start.29 = (bf16[512,256]{1,0:T(8,128)(2,1)S(1)}, bf16[512,256]{1,0:T(8,128)(2,1)S(1)}, u32[]{:S(2)}, u32[]{:S(2)}) collective-permute-start(bf16[512,256]{1,0:T(8,128)(2,1)S(1)} %add_convert_fusion.5), channel_id=1, source_target_pairs={{8,0},{16,8},{24,16},{28,24},{20,28},{12,20},{4,12},{0,4},{9,1},{1... | collective-permute-start | bytes 786440 | tf_op jit(solution)/shard_map/ppermute | solution.py:294
  39.1 13.3 %collective-permute-start.19 = (bf16[512,256]{1,0:T(8,128)(2,1)S(1)}, bf16[512,256]{1,0:T(8,128)(2,1)S(1)}, u32[]{:S(2)}, u32[]{:S(2)}) collective-permute-start(bf16[512,256]{1,0:T(8,128)(2,1)S(1)} %convert_element_type.108), channel_id=1, source_target_pairs={{0,8},{8,16},{16,24},{24,28},{28,20},{20,12},{12,4},{4,0},{1,9},{9... | collective-permute-start | bytes 786440 | tf_op jit(solution)/shard_map/ppermute | solution.py:294
  43.4 13.5 %collective-permute-start.11 = (bf16[528,256]{1,0:T(8,128)(2,1)S(1)}, bf16[528,256]{1,0:T(8,128)(2,1)S(1)}, u32[]{:S(2)}, u32[]{:S(2)}) collective-permute-start(bf16[528,256]{1,0:T(8,128)(2,1)S(1)} %collective-permute-done.10.q), channel_id=1, source_target_pairs={{0,8},{8,16},{16,24},{24,28},{28,20},{20,12},{12,4},{4,0},{1,9},{9... | collective-permute-start | bytes 811016 | tf_op jit(solution)/shard_map/ppermute | solution.py:278
  48.8 12.1 %collective-permute-start.8 = (bf16[528,256]{1,0:T(8,128)(2,1)S(1)}, bf16[528,256]{1,0:T(8,128)(2,1)S(1)}, u32[]{:S(2)}, u32[]{:S(2)}) collective-permute-start(bf16[528,256]{1,0:T(8,128)(2,1)S(1)} %collective-permute-done.7.q), channel_id=1, source_target_pairs={{8,0},{16,8},{24,16},{28,24},{20,28},{12,20},{4,12},{0,4},{9,1},{1... | collective-permute-start | bytes 811016 | tf_op jit(solution)/shard_map/ppermute | solution.py:278
  52.1 11.7 %collective-permute-start.30 = (bf16[512,256]{1,0:T(8,128)(2,1)S(1)}, bf16[512,256]{1,0:T(8,128)(2,1)S(1)}, u32[]{:S(2)}, u32[]{:S(2)}) collective-permute-start(bf16[512,256]{1,0:T(8,128)(2,1)S(1)} %add_convert_fusion.4), channel_id=1, source_target_pairs={{8,0},{16,8},{24,16},{28,24},{20,28},{12,20},{4,12},{0,4},{9,1},{1... | collective-permute-start | bytes 786440 | tf_op jit(solution)/shard_map/ppermute | solution.py:294
  52.5 11.7 %collective-permute-start.20 = (bf16[512,256]{1,0:T(8,128)(2,1)S(1)}, bf16[512,256]{1,0:T(8,128)(2,1)S(1)}, u32[]{:S(2)}, u32[]{:S(2)}) collective-permute-start(bf16[512,256]{1,0:T(8,128)(2,1)S(1)} %add_convert_fusion.11), channel_id=1, source_target_pairs={{0,8},{8,16},{16,24},{24,28},{28,20},{20,12},{12,4},{4,0},{1,9},{9... | collective-permute-start | bytes 786440 | tf_op jit(solution)/shard_map/ppermute | solution.py:294
  59.3 9.2 %collective-permute-start.12 = (bf16[528,256]{1,0:T(8,128)(2,1)S(1)}, bf16[528,256]{1,0:T(8,128)(2,1)S(1)}, u32[]{:S(2)}, u32[]{:S(2)}) collective-permute-start(bf16[528,256]{1,0:T(8,128)(2,1)S(1)} %collective-permute-done.11.q), channel_id=1, source_target_pairs={{0,8},{8,16},{16,24},{24,28},{28,20},{20,12},{12,4},{4,0},{1,9},{9... | collective-permute-start | bytes 811016 | tf_op jit(solution)/shard_map/ppermute | solution.py:278
  63.3 9.2 %collective-permute-start.16 = (bf16[528,256]{1,0:T(8,128)(2,1)S(1)}, bf16[528,256]{1,0:T(8,128)(2,1)S(1)}, u32[]{:S(2)}, u32[]{:S(2)}) collective-permute-start(bf16[528,256]{1,0:T(8,128)(2,1)S(1)} %collective-permute-done.8.q), channel_id=1, source_target_pairs={{8,0},{16,8},{24,16},{28,24},{20,28},{12,20},{4,12},{0,4},{9,1},{1... | collective-permute-start | bytes 811016 | tf_op jit(solution)/shard_map/ppermute | solution.py:278
  63.9 11.5 %collective-permute-start.31 = (bf16[512,256]{1,0:T(8,128)(2,1)S(1)}, bf16[512,256]{1,0:T(8,128)(2,1)S(1)}, u32[]{:S(2)}, u32[]{:S(2)}) collective-permute-start(bf16[512,256]{1,0:T(8,128)(2,1)S(1)} %add_convert_fusion.3), channel_id=1, source_target_pairs={{8,0},{16,8},{24,16},{28,24},{20,28},{12,20},{4,12},{0,4},{9,1},{1... | collective-permute-start | bytes 786440 | tf_op jit(solution)/shard_map/ppermute | solution.py:294
  64.2 11.9 %collective-permute-start.21 = (bf16[512,256]{1,0:T(8,128)(2,1)S(1)}, bf16[512,256]{1,0:T(8,128)(2,1)S(1)}, u32[]{:S(2)}, u32[]{:S(2)}) collective-permute-start(bf16[512,256]{1,0:T(8,128)(2,1)S(1)} %add_convert_fusion.10), channel_id=1, source_target_pairs={{0,8},{8,16},{16,24},{24,28},{28,20},{20,12},{12,4},{4,0},{1,9},{9... | collective-permute-start | bytes 786440 | tf_op jit(solution)/shard_map/ppermute | solution.py:294
  70.8 8.7 %collective-permute-start.13 = (bf16[528,256]{1,0:T(8,128)(2,1)S(1)}, bf16[528,256]{1,0:T(8,128)(2,1)S(1)}, u32[]{:S(2)}, u32[]{:S(2)}) collective-permute-start(bf16[528,256]{1,0:T(8,128)(2,1)S(1)} %collective-permute-done.12.q), channel_id=1, source_target_pairs={{0,8},{8,16},{16,24},{24,28},{28,20},{20,12},{12,4},{4,0},{1,9},{9... | collective-permute-start | bytes 811016 | tf_op jit(solution)/shard_map/ppermute | solution.py:278
  74.9 9.1 %collective-permute-start.17 = (bf16[528,256]{1,0:T(8,128)(2,1)S(1)}, bf16[528,256]{1,0:T(8,128)(2,1)S(1)}, u32[]{:S(2)}, u32[]{:S(2)}) collective-permute-start(bf16[528,256]{1,0:T(8,128)(2,1)S(1)} %collective-permute-done.16.q), channel_id=1, source_target_pairs={{8,0},{16,8},{24,16},{28,24},{20,28},{12,20},{4,12},{0,4},{9,1},{1... | collective-permute-start | bytes 811016 | tf_op jit(solution)/shard_map/ppermute | solution.py:278
  75.4 11.2 %collective-permute-start.32 = (bf16[512,256]{1,0:T(8,128)(2,1)S(1)}, bf16[512,256]{1,0:T(8,128)(2,1)S(1)}, u32[]{:S(2)}, u32[]{:S(2)}) collective-permute-start(bf16[512,256]{1,0:T(8,128)(2,1)S(1)} %add_convert_fusion.2), channel_id=1, source_target_pairs={{8,0},{16,8},{24,16},{28,24},{20,28},{12,20},{4,12},{0,4},{9,1},{1... | collective-permute-start | bytes 786440 | tf_op jit(solution)/shard_map/ppermute | solution.py:294
  76.2 12.0 %collective-permute-start.22 = (bf16[512,256]{1,0:T(8,128)(2,1)S(1)}, bf16[512,256]{1,0:T(8,128)(2,1)S(1)}, u32[]{:S(2)}, u32[]{:S(2)}) collective-permute-start(bf16[512,256]{1,0:T(8,128)(2,1)S(1)} %add_convert_fusion.9), channel_id=1, source_target_pairs={{0,8},{8,16},{16,24},{24,28},{28,20},{20,12},{12,4},{4,0},{1,9},{9... | collective-permute-start | bytes 786440 | tf_op jit(solution)/shard_map/ppermute | solution.py:294
  81.9 9.7 %collective-permute-start.14 = (bf16[528,256]{1,0:T(8,128)(2,1)S(1)}, bf16[528,256]{1,0:T(8,128)(2,1)S(1)}, u32[]{:S(2)}, u32[]{:S(2)}) collective-permute-start(bf16[528,256]{1,0:T(8,128)(2,1)S(1)} %collective-permute-done.13.q), channel_id=1, source_target_pairs={{0,8},{8,16},{16,24},{24,28},{28,20},{20,12},{12,4},{4,0},{1,9},{9... | collective-permute-start | bytes 811016 | tf_op jit(solution)/shard_map/ppermute | solution.py:278
  86.4 9.2 %collective-permute-start.18 = (bf16[528,256]{1,0:T(8,128)(2,1)S(1)}, bf16[528,256]{1,0:T(8,128)(2,1)S(1)}, u32[]{:S(2)}, u32[]{:S(2)}) collective-permute-start(bf16[528,256]{1,0:T(8,128)(2,1)S(1)} %collective-permute-done.17.q), channel_id=1, source_target_pairs={{8,0},{16,8},{24,16},{28,24},{20,28},{12,20},{4,12},{0,4},{9,1},{1... | collective-permute-start | bytes 811016 | tf_op jit(solution)/shard_map/ppermute | solution.py:278
  86.7 11.3 %collective-permute-start.33 = (bf16[512,256]{1,0:T(8,128)(2,1)S(1)}, bf16[512,256]{1,0:T(8,128)(2,1)S(1)}, u32[]{:S(2)}, u32[]{:S(2)}) collective-permute-start(bf16[512,256]{1,0:T(8,128)(2,1)S(1)} %add_convert_fusion.1), channel_id=1, source_target_pairs={{8,0},{16,8},{24,16},{28,24},{20,28},{12,20},{4,12},{0,4},{9,1},{1... | collective-permute-start | bytes 786440 | tf_op jit(solution)/shard_map/ppermute | solution.py:294
  88.3 10.3 %collective-permute-start.23 = (bf16[512,256]{1,0:T(8,128)(2,1)S(1)}, bf16[512,256]{1,0:T(8,128)(2,1)S(1)}, u32[]{:S(2)}, u32[]{:S(2)}) collective-permute-start(bf16[512,256]{1,0:T(8,128)(2,1)S(1)} %add_convert_fusion.8), channel_id=1, source_target_pairs={{0,8},{8,16},{16,24},{24,28},{28,20},{20,12},{12,4},{4,0},{1,9},{9... | collective-permute-start | bytes 786440 | tf_op jit(solution)/shard_map/ppermute | solution.py:294
  94.0 8.1 %collective-permute-start.15 = (bf16[528,256]{1,0:T(8,128)(2,1)S(1)}, bf16[528,256]{1,0:T(8,128)(2,1)S(1)}, u32[]{:S(2)}, u32[]{:S(2)}) collective-permute-start(bf16[528,256]{1,0:T(8,128)(2,1)S(1)} %collective-permute-done.14.q), channel_id=1, source_target_pairs={{0,8},{8,16},{16,24},{24,28},{28,20},{20,12},{12,4},{4,0},{1,9},{9... | collective-permute-start | bytes 811016 | tf_op jit(solution)/shard_map/ppermute | solution.py:278
  98.0 6.5 %copy-start.1 = (bf16[256,1024]{1,0:T(8,128)(2,1)S(1)}, bf16[256,1024]{1,0:T(8,128)(2,1)}, u32[]{:S(2)}) copy-start(bf16[256,1024]{1,0:T(8,128)(2,1)} %w_out.3) | copy-start | bytes 1572868
  98.1 6.4 %collective-permute-start.34 = (bf16[512,256]{1,0:T(8,128)(2,1)S(1)}, bf16[512,256]{1,0:T(8,128)(2,1)S(1)}, u32[]{:S(2)}, u32[]{:S(2)}) collective-permute-start(bf16[512,256]{1,0:T(8,128)(2,1)S(1)} %add_convert_fusion), channel_id=1, source_target_pairs={{8,0},{16,8},{24,16},{28,24},{20,28},{12,20},{4,12},{0,4},{9,1},{1... | collective-permute-start | bytes 786440 | tf_op jit(solution)/shard_map/ppermute | solution.py:294
  98.7 6.5 %collective-permute-start.24 = (bf16[512,256]{1,0:T(8,128)(2,1)S(1)}, bf16[512,256]{1,0:T(8,128)(2,1)S(1)}, u32[]{:S(2)}, u32[]{:S(2)}) collective-permute-start(bf16[512,256]{1,0:T(8,128)(2,1)S(1)} %add_convert_fusion.7), channel_id=1, source_target_pairs={{0,8},{8,16},{16,24},{24,28},{28,20},{20,12},{12,4},{4,0},{1,9},{9... | collective-permute-start | bytes 786440 | tf_op jit(solution)/shard_map/ppermute | solution.py:294
  104.4 24.7 %copy-start.4 = (bf16[1024,256]{1,0:T(8,128)(2,1)S(1)}, bf16[1024,256]{1,0:T(8,128)(2,1)}, u32[]{:S(2)}) copy-start(bf16[1024,256]{1,0:T(8,128)(2,1)} %param.10) | copy-start | bytes 1572868
  105.0 9.5 %collective-permute-start.35 = (bf16[2,512,256]{2,1,0:T(8,128)(2,1)S(1)}, bf16[2,512,256]{2,1,0:T(8,128)(2,1)S(1)}, u32[]{:S(2)}, u32[]{:S(2)}) collective-permute-start(bf16[2,512,256]{2,1,0:T(8,128)(2,1)S(1)} %get-tuple-element.58), channel_id=1, source_target_pairs={{0,1},{1,0},{2,3},{3,2},{4,5},{5,4},{6,7},{7,6},{8,9},{9,8},{10,11... | collective-permute-start | bytes 1572872 | tf_op jit(solution)/shard_map/ppermute | solution.py:239
  105.2 8.8 %collective-permute-start.25 = (bf16[512,256]{1,0:T(8,128)(2,1)S(1)}, bf16[512,256]{1,0:T(8,128)(2,1)S(1)}, u32[]{:S(2)}, u32[]{:S(2)}) collective-permute-start(bf16[512,256]{1,0:T(8,128)(2,1)S(1)} %add_convert_fusion.6), channel_id=1, source_target_pairs={{0,8},{8,16},{16,24},{24,28},{28,20},{20,12},{12,4},{4,0},{1,9},{9... | collective-permute-start | bytes 786440 | tf_op jit(solution)/shard_map/ppermute | solution.py:294
  114.5 2.0 %collective-permute-start.26 = (bf16[2,512,256]{2,1,0:T(8,128)(2,1)S(1)}, bf16[2,512,256]{2,1,0:T(8,128)(2,1)S(1)}, u32[]{:S(2)}, u32[]{:S(2)}) collective-permute-start(bf16[2,512,256]{2,1,0:T(8,128)(2,1)S(1)} %get-tuple-element.56), channel_id=1, source_target_pairs={{0,1},{1,0},{2,3},{3,2},{4,5},{5,4},{6,7},{7,6},{8,9},{9,8},{10,11... | collective-permute-start | bytes 1572872 | tf_op jit(solution)/shard_map/ppermute | solution.py:239
  114.7 9.2 %collective-permute-start.36 = (bf16[1,512,256]{2,1,0:T(8,128)(2,1)S(1)}, bf16[1,512,256]{2,1,0:T(8,128)(2,1)S(1)}, u32[]{:S(2)}, u32[]{:S(2)}) collective-permute-start(bf16[1,512,256]{2,1,0:T(8,128)(2,1)S(1)} %slice.52), channel_id=1, source_target_pairs={{0,2},{1,3},{2,0},{3,1},{4,6},{5,7},{6,4},{7,5},{8,10},{9,11},{10,... | collective-permute-start | bytes 786440 | tf_op jit(solution)/shard_map/ppermute | solution.py:239
  116.7 12.4 %collective-permute-start.27 = (bf16[1,512,256]{2,1,0:T(8,128)(2,1)S(1)}, bf16[1,512,256]{2,1,0:T(8,128)(2,1)S(1)}, u32[]{:S(2)}, u32[]{:S(2)}) collective-permute-start(bf16[1,512,256]{2,1,0:T(8,128)(2,1)S(1)} %slice.53), channel_id=1, source_target_pairs={{0,2},{1,3},{2,0},{3,1},{4,6},{5,7},{6,4},{7,5},{8,10},{9,11},{10,... | collective-permute-start | bytes 786440 | tf_op jit(solution)/shard_map/ppermute | solution.py:239

commit v2 on v1

--- a/solution.py
+++ b/solution.py
@@ -2,7 +2,6 @@
 
 import jax
 import jax.numpy as jnp
-import numpy as np
 from jax import lax
 from jax.experimental import pallas as pl
 from jax.experimental.pallas import tpu as pltpu
@@ -52,37 +51,43 @@
     return value * (0.5 + 0.5 * jnp.tanh(0.5 * value))
 
 
-def near_kernel(first, second, mate, w_in, cache, partial, w_here, cache_here, sems):
-    copies = [
-        pltpu.make_async_copy(source, target, sems.at[i])
-        for i, (source, target) in enumerate(((w_in, w_here), (cache, cache_here)))
-    ]
+def near_kernel(
+    slots, feats, mate, w_in, cache, event_mask, partial, w_here, cache_here, live, sems
+):
+    peers, cap = slots.shape
+    copies = [pltpu.make_async_copy(w_in, w_here, sems.at[peers * cap])]
+    for i in range(peers * cap):
+        slot = slots[i // cap, i % cap]
+        copies.append(pltpu.make_async_copy(cache.at[slot], cache_here.at[i], sems.at[i]))
     for copy in copies:
         copy.start()
+    for i in range(peers * cap):
+        live[i : i + 1] = event_mask[pl.ds(slots[i // cap, i % cap], 1)]
     copies[0].wait()
-    half, width = first.shape
+    width = feats.shape[1]
     part = lax.axis_index("tp")
-    own, other = (
-        w_here[pl.ds(pl.multiple_of((part ^ m) * width, width), width)] for m in range(2)
-    )
-    for begin, piece in ((0, first), (half, second)):
-        rows = slice(begin, begin + half)
-        partial[rows] = jnp.dot(
-            piece[...], own, preferred_element_type=jnp.float32
-        ) + jnp.dot(mate[rows], other, preferred_element_type=jnp.float32)
-    copies[1].wait()
-
-
-def near(first, second, mate, w_in, cache):
+    total = None
+    for m, piece in enumerate((feats, mate)):
+        start = pl.multiple_of((part ^ m) * width, width)
+        term = jnp.dot(
+            piece[...], w_here[pl.ds(start, width)], preferred_element_type=jnp.float32
+        )
+        total = term if total is None else total + term
+    partial[...] = total
+    for copy in copies[1:]:
+        copy.wait()
+
+
+def near(slots, feats, mate, w_in, cache, event_mask):
     rows, width = mate.shape
     hbm = pl.BlockSpec(memory_space=pltpu.HBM)
-    held = [jax.ShapeDtypeStruct(value.shape, value.dtype) for value in (w_in, cache)]
+    held = [jax.ShapeDtypeStruct(value.shape, value.dtype) for value in (w_in, cache, event_mask)]
     return pl.pallas_call(
         near_kernel,
         out_shape=(jax.ShapeDtypeStruct((rows, w_in.shape[1]), jnp.float32), *held),
-        in_specs=[VMEM] * 3 + [hbm] * 2,
-        out_specs=(VMEM,) * 3,
-        scratch_shapes=[pltpu.SemaphoreType.DMA((2,))],
+        in_specs=[SMEM] + [VMEM] * 2 + [hbm] * 2 + [VMEM],
+        out_specs=(VMEM,) * 4,
+        scratch_shapes=[pltpu.SemaphoreType.DMA((cache.shape[0] + 1,))],
         compiler_params=pltpu.CompilerParams(vmem_limit_bytes=8 * 1024 * 1024),
         cost_estimate=pl.CostEstimate(
             flops=4 * rows * width * w_in.shape[1],
@@ -90,12 +95,12 @@
             transcendentals=0,
         ),
         name="near",
-    )(pin(first), pin(second), pin(mate), in_hbm(w_in), in_hbm(cache))
+    )(slots, pin(feats), pin(mate), in_hbm(w_in), in_hbm(cache), pin(event_mask))
 
 
 def project_kernel(heads, gate, begin, first, partial, *refs):
     slices, (w_in, facts, out) = refs[:-3], refs[-3:]
-    rows, width = slices[0].shape
+    rows, width = partial.shape[0] // 2, slices[0].shape[1]
     part = lax.axis_index("tp")
     for h in range(heads):
         column = (2 * h + gate) * DH
@@ -103,7 +108,7 @@
         for m, piece in enumerate(slices):
             start = pl.multiple_of((part ^ (m + first)) * width, width)
             total += jnp.dot(
-                piece[...],
+                piece[begin : begin + rows],
                 w_in[pl.ds(start, width), column : column + DH],
                 preferred_element_type=jnp.float32,
             )
@@ -112,8 +117,7 @@
         out[rows:] = facts[...]
 
 
-def project(partial, slices, w_in, facts, heads, gate, begin, first):
-    rows = slices[0].shape[0]
+def project(partial, slices, w_in, facts, heads, gate, begin, rows, first):
     return pl.pallas_call(
         functools.partial(project_kernel, heads, gate, begin, first),
         out_shape=jax.ShapeDtypeStruct(
@@ -126,10 +130,10 @@
     )(pin(partial), *[pin(piece) for piece in slices], pin(w_in), pin(facts))
 
 
-def attend_kernel(heads, cap, step, begin, route, slots, event_mask, q, cache, out):
+def attend_kernel(heads, cap, begin, met, live, q, cache, out):
     rows, width = out.shape
     me = lax.axis_index("user")
-    index = route[me, step]
+    index = sum(jnp.where(me == place, other, 0) for place, other in enumerate(met))
     labels = lax.broadcasted_iota(jnp.int32, (DH, EVENTS), 0)
 
     facts = q[rows:].astype(jnp.float32).astype(jnp.int32)
@@ -143,11 +147,11 @@
     line = 2 * rows // width
     owners = facts[line : line + 1, :DH]
     lanes = lax.broadcasted_iota(jnp.int32, (1, DH), 1)
+    events = live[index]
     penalty = []
     for c in range(cap):
         owner = jnp.sum(jnp.where(lanes == me * cap + c, owners, 0), axis=1, keepdims=True)
-        live = event_mask[pl.ds(slots[index, c], 1)] > 0
-        label = jnp.where(live, owner, -1)
+        label = jnp.where(events[c : c + 1] > 0, owner, -1)
         penalty.append(jnp.where(label == labels, 0.0, MASKED).T.astype(jnp.bfloat16))
 
     per = min(2, cap)
@@ -155,7 +159,7 @@
         left = jnp.concatenate([q[:rows, h * DH : (h + 1) * DH], hot], axis=1)
         total = None
         for c in range(0, cap, per):
-            held = [cache.at[slots[index, c + i]] for i in range(per)]
+            held = [cache.at[index * cap + c + i] for i in range(per)]
             keys = jnp.concatenate([b[:, 2 * h * DH : (2 * h + 1) * DH] for b in held], axis=0)
             values = jnp.concatenate(
                 [b[:, (2 * h + 1) * DH : (2 * h + 2) * DH] for b in held], axis=0
@@ -170,16 +174,16 @@
         out[:, h * DH : (h + 1) * DH] = total
 
 
-def attend(step, begin, route, slots, event_mask, q, cache, heads, cap):
+def attend(begin, met, live, q, cache, heads, cap):
     rows = q.shape[0] - FACT_ROWS
     return pl.pallas_call(
-        functools.partial(attend_kernel, heads, cap, step, begin),
+        functools.partial(attend_kernel, heads, cap, begin, met),
         out_shape=jax.ShapeDtypeStruct((rows, heads * DH), jnp.float32),
-        in_specs=[SMEM] * 2 + [VMEM] * 3,
+        in_specs=[VMEM] * 3,
         out_specs=VMEM,
         compiler_params=pltpu.CompilerParams(vmem_limit_bytes=8 * 1024 * 1024),
         name="attend",
-    )(route, slots, pin(event_mask), pin(q), pin(cache))
+    )(pin(live), pin(q), pin(cache))
 
 
 def finish_kernel(heads, parts, own, arrived, gates, w_out, sent, kept):
@@ -228,10 +232,10 @@
     half = row_count // 2
 
     order = ring_order(peers)
-    route = np.zeros((peers, peers), np.int32)
+    route = [[0] * peers for _ in range(peers)]
     for position, index in enumerate(order):
-        route[index] = [order[(position - step) % peers] for step in range(peers)]
-    route = jnp.array(route)
+        for step in range(peers):
+            route[step][index] = order[(position - step) % peers]
     onward = [(order[i], order[(i + 1) % peers]) for i in range(peers)]
     back = [(b, a) for a, b in onward]
 
@@ -249,27 +253,23 @@
     facts = jnp.concatenate([users, owners], axis=0).astype(jnp.bfloat16)
     facts = jnp.pad(facts, ((0, FACT_ROWS - facts.shape[0]), (0, 0)))
 
-    rows = {begin: cand_feats[begin : begin + half] for begin in begins}
     mate, facts = lax.optimization_barrier((swap(cand_feats, "tp", 1), facts))
-    partial, w_in, cache = near(rows[0], rows[half], mate, w_in, kv_cache)
+    partial, w_in, cache, live = near(send_slots, cand_feats, mate, w_in, kv_cache, event_mask)
+    live = live.reshape(peers, cap, EVENTS)
+    far = {0: cand_feats}
+    for bit in reversed(bits(parts)[1:]):
+        far.update({m | bit: swap(value, "tp", bit) for m, value in far.items()})
+    del far[0]
+    far, _ = lax.optimization_barrier((far, partial))
+    far.update({m | 1: swap(value, "tp", 1) for m, value in far.items()})
+    far = [far[m] for m in range(2, parts)]
     queries, gates = {}, {}
-    last = partial
     for begin in begins:
-        far = {0: rows[begin]}
-        if begin != begins[0]:
-            far, _ = lax.optimization_barrier((far, partial))
-        for bit in reversed(bits(parts)[1:]):
-            far.update({m | bit: swap(value, "tp", bit) for m, value in far.items()})
-        del far[0]
-        far, last = lax.optimization_barrier((far, last))
-        far.update({m | 1: swap(value, "tp", 1) for m, value in far.items()})
-        far = [far[m] for m in range(2, parts)]
-        queries[begin] = project(partial, far, w_in, facts, heads, 0, begin, 2)
-        gates[begin] = project(partial, far, w_in, facts, heads, 1, begin, 2)
-        last = queries[begin]
+        queries[begin] = project(partial, far, w_in, facts, heads, 0, begin, half, 2)
+        gates[begin] = project(partial, far, w_in, facts, heads, 1, begin, half, 2)
 
     def score(step, begin, query):
-        return attend(step, begin, route, send_slots, event_mask, query, cache, heads, cap)
+        return attend(begin, route[step], live, query, cache, heads, cap)
 
     way = {0: onward, half: back}
     queries_at = {begin: [queries[begin]] for begin in begins}
@@ -299,7 +299,7 @@
         for bit in bits(parts):
             total = kept + swap(sent, "tp", bit).astype(jnp.float32)
             sent, kept = total[1::2].astype(jnp.bfloat16), total[::2]
-        scored[begin] = (rows[begin].astype(jnp.float32) + total[0]).astype(jnp.bfloat16)
+        scored[begin] = (cand_feats[begin : begin + half].astype(jnp.float32) + total[0]).astype(jnp.bfloat16)
     return jnp.concatenate([scored[0], scored[half]], axis=0)
 
 

time: 130 us -> 130 us (level)
  Pallas kernels: 44.6 us -> 35.3 us
  waiting for transfers between devices: 37.9 us -> 45.8 us
  local copies, waits for them, and re-layouts: 1.18 us -> 2.57 us
    pallas_call x16, Pallas kernels: 38 us -> 27.7 us  [attend(): pl.pallas_call(functools.partial(attend_kernel, heads, cap, begin, met),...]
    ppermute x14, waiting for transfers between devices: 9.78 us -> 19 us  [per_device(): sums[begin] = lax.ppermute(term.astype(jnp.bfloat16), 'user', way[begin])]
    unnamed x10, local copies, waits for them, and re-layouts: 0.03 us -> 2.49 us
    ppermute x9 -> x7, waiting for transfers between devices: 18.1 us -> 15.9 us  [swap(): lax.ppermute(value, axis, [(i, i ^ bit) for i in range(lax.axis_size(axis...]
    ppermute x9 -> x7, starting transfers between devices: 8.45 us -> 6.6 us  [swap(): lax.ppermute(value, axis, [(i, i ^ bit) for i in range(lax.axis_size(axis...]
    ppermute x14, starting transfers between devices: 16.8 us -> 18.6 us  [per_device(): lax.ppermute(queries_at[begin][-1], 'user', way[begin])]
  transfers between devices with their start and end apart: 37 -> 35, of which waited for: 15 -> 17; matrix products, arithmetic and copies ran while one was open for 3% -> 3% of each run, Pallas kernels for 34% -> 27%
where the time goes in v2:
time: 130 us
  waiting for transfers between devices  45.8 us (35%)
  starting transfers between devices  41.3 us (32%)
  Pallas kernels  35.3 us (27%)
  other arithmetic  4.24 us (3%)
  local copies, waits for them, and re-layouts  2.57 us (2%)
    pallas_call x16, Pallas kernels, attend(): pl.pallas_call(functools.partial(attend_kernel, heads, cap, begin, met),...  27.7 us
    ppermute x14, waiting for transfers between devices, per_device(): sums[begin] = lax.ppermute(term.astype(jnp.bfloat16), 'user', way[begin])  19 us
    ppermute x14, starting transfers between devices, per_device(): lax.ppermute(queries_at[begin][-1], 'user', way[begin])  18.6 us
    ppermute x14, starting transfers between devices, per_device(): sums[begin] = lax.ppermute(term.astype(jnp.bfloat16), 'user', way[begin])  16.2 us
    ppermute x7, waiting for transfers between devices, swap(): lax.ppermute(value, axis, [(i, i ^ bit) for i in range(lax.axis_size(axis...  15.9 us
    ppermute x14, waiting for transfers between devices, per_device(): lax.ppermute(queries_at[begin][-1], 'user', way[begin])  11 us
    ppermute x7, starting transfers between devices, swap(): lax.ppermute(value, axis, [(i, i ^ bit) for i in range(lax.axis_size(axis...  6.6 us
    pallas_call x1, Pallas kernels, near(): pl.pallas_call(near_kernel, out_shape=(jax.ShapeDtypeStruct((rows, w_in.s...  4.82 us
  transfers between devices with their start and end apart: 35, of which 17 were waited for; matrix products, arithmetic and copies ran while one was open for 3% of the time, Pallas kernels for 27%

profile of v2, /device:TPU:0, one launch (start us, length us, event | category | flops | bytes accessed | tf_op | source)
XLA Modules:
  0.0 129.7 jit_solution(16180467705537726231)
XLA Ops:
  0.5 2.5 %collective-permute-start.1 = (bf16[1024,256]{1,0:T(8,128)(2,1)}, bf16[1024,256]{1,0:T(8,128)(2,1)S(1)}, u32[]{:S(2)}, u32[]{:S(2)}) collective-permute-start(bf16[1024,256]{1,0:T(8,128)(2,1)} %feats.1), channel_id=1, source_target_pairs={{0,2},{1,3},{2,0},{3,1},{4,6},{5,7},{6,4},{7,5},{8,10},{9,11},{10,... | collective-permute-start | bytes 1572872 | tf_op jit(solution)/shard_map/ppermute | solution.py:243
  7.7 4.8 %near.1 = (f32[1024,512]{1,0:T(8,128)S(1)}, bf16[1024,512]{1,0:T(8,128)(2,1)S(1)}, bf16[64,128,512]{2,1,0:T(8,128)(2,1)S(1)}, s32[64,128]{1,0:T(8,128)S(1)}) custom-call(s32[8,8]{1,0:T(8,128)S(1)} %copy-done.4, bf16[1024,256]{1,0:T(8,128)(2,1)S(1)} %copy-done.1, bf16[1024,256]{1,0:T(8,128)(2,1)S(1)} %collective-permute-done.mate, bf16[1024,512]{1,0:T(8,128)(2,1)} %w_in.1, ...), custom_call_target="tpu_custom_call" | custom-call | flops 536870912 | bytes 10485760 | tf_op jit(solution)/shard_map/near/pallas_call | solution.py:85
  12.6 3.2 %collective-permute-done.1.refs_0_ = bf16[1024,256]{1,0:T(8,128)(2,1)S(1)} collective-permute-done((bf16[1024,256]{1,0:T(8,128)(2,1)}, bf16[1024,256]{1,0:T(8,128)(2,1)S(1)}, u32[]{:S(2)}, u32[]{:S(2)}) %collective-permute-start.1) | collective-permute-done | bytes 524320 | tf_op jit(solution)/shard_map/ppermute | solution.py:243
  15.8 1.9 %collective-permute-done.2.refs_1_ = bf16[1024,256]{1,0:T(8,128)(2,1)S(1)} collective-permute-done((bf16[1024,256]{1,0:T(8,128)(2,1)S(1)}, bf16[1024,256]{1,0:T(8,128)(2,1)S(1)}, u32[]{:S(2)}, u32[]{:S(2)}) %collective-permute-start.2) | collective-permute-done | bytes 524320 | tf_op jit(solution)/shard_map/ppermute | solution.py:243
  18.1 1.8 %collective-permute-start.3 = (bf16[528,256]{1,0:T(8,128)(2,1)S(1)}, bf16[528,256]{1,0:T(8,128)(2,1)S(1)}, u32[]{:S(2)}, u32[]{:S(2)}) collective-permute-start(bf16[528,256]{1,0:T(8,128)(2,1)S(1)} %queries.3.q), channel_id=1, source_target_pairs={{8,0},{16,8},{24,16},{28,24},{20,28},{12,20},{4,12},{0,4},{9,1},{1... | collective-permute-start | bytes 811016 | tf_op jit(solution)/shard_map/ppermute | solution.py:278
  20.7 6.0 %collective-permute-done.3.q = bf16[528,256]{1,0:T(8,128)(2,1)S(1)} collective-permute-done((bf16[528,256]{1,0:T(8,128)(2,1)S(1)}, bf16[528,256]{1,0:T(8,128)(2,1)S(1)}, u32[]{:S(2)}, u32[]{:S(2)}) %collective-permute-start.3) | collective-permute-done | bytes 270368 | tf_op jit(solution)/shard_map/ppermute | solution.py:278
  26.8 1.7 %collective-permute-start.4 = (bf16[528,256]{1,0:T(8,128)(2,1)S(1)}, bf16[528,256]{1,0:T(8,128)(2,1)S(1)}, u32[]{:S(2)}, u32[]{:S(2)}) collective-permute-start(bf16[528,256]{1,0:T(8,128)(2,1)S(1)} %collective-permute-done.3.q), channel_id=1, source_target_pairs={{8,0},{16,8},{24,16},{28,24},{20,28},{12,20},{4,12},{0,4},{9,1},{1... | collective-permute-start | bytes 811016 | tf_op jit(solution)/shard_map/ppermute | solution.py:278
  28.4 1.7 %attend.16 = f32[512,256]{1,0:T(8,128)S(1)} custom-call(s32[8,8,128]{2,1,0:T(8,128)S(1)} %bitcast.13, bf16[528,256]{1,0:T(8,128)(2,1)S(1)} %collective-permute-done.3.q, bf16[64,128,512]{2,1,0:T(8,128)(2,1)S(1)} %get-tuple-element.37.cache), custom_call_target="tpu_custom_call" | custom-call | tf_op jit(solution)/shard_map/attend/pallas_call | solution.py:179
  30.2 1.6 %collective-permute-start.26 = (bf16[512,256]{1,0:T(8,128)(2,1)S(1)}, bf16[512,256]{1,0:T(8,128)(2,1)S(1)}, u32[]{:S(2)}, u32[]{:S(2)}) collective-permute-start(bf16[512,256]{1,0:T(8,128)(2,1)S(1)} %convert_element_type.125), channel_id=1, source_target_pairs={{8,0},{16,8},{24,16},{28,24},{20,28},{12,20},{4,12},{0,4},{9,1},{1... | collective-permute-start | bytes 786440 | tf_op jit(solution)/shard_map/ppermute | solution.py:294
  31.8 1.7 %attend.17 = f32[512,256]{1,0:T(8,128)S(1)} custom-call(s32[8,8,128]{2,1,0:T(8,128)S(1)} %bitcast.14, bf16[528,256]{1,0:T(8,128)(2,1)S(1)} %collective-permute-done.7.q, bf16[64,128,512]{2,1,0:T(8,128)(2,1)S(1)} %get-tuple-element.37.cache), custom_call_target="tpu_custom_call" | custom-call | tf_op jit(solution)/shard_map/attend/pallas_call | solution.py:179
  34.1 2.1 %collective-permute-done.4.q = bf16[528,256]{1,0:T(8,128)(2,1)S(1)} collective-permute-done((bf16[528,256]{1,0:T(8,128)(2,1)S(1)}, bf16[528,256]{1,0:T(8,128)(2,1)S(1)}, u32[]{:S(2)}, u32[]{:S(2)}) %collective-permute-start.4) | collective-permute-done | bytes 270368 | tf_op jit(solution)/shard_map/ppermute | solution.py:278
  36.2 1.7 %attend.18 = f32[512,256]{1,0:T(8,128)S(1)} custom-call(s32[8,8,128]{2,1,0:T(8,128)S(1)} %bitcast.15, bf16[528,256]{1,0:T(8,128)(2,1)S(1)} %collective-permute-done.4.q, bf16[64,128,512]{2,1,0:T(8,128)(2,1)S(1)} %get-tuple-element.37.cache), custom_call_target="tpu_custom_call" | custom-call | tf_op jit(solution)/shard_map/attend/pallas_call | solution.py:179
  37.9 1.7 %collective-permute-start.5 = (bf16[528,256]{1,0:T(8,128)(2,1)S(1)}, bf16[528,256]{1,0:T(8,128)(2,1)S(1)}, u32[]{:S(2)}, u32[]{:S(2)}) collective-permute-start(bf16[528,256]{1,0:T(8,128)(2,1)S(1)} %collective-permute-done.4.q), channel_id=1, source_target_pairs={{8,0},{16,8},{24,16},{28,24},{20,28},{12,20},{4,12},{0,4},{9,1},{1... | collective-permute-start | bytes 811016 | tf_op jit(solution)/shard_map/ppermute | solution.py:278
  39.6 2.2 %collective-permute-done.26 = bf16[512,256]{1,0:T(8,128)(2,1)S(1)} collective-permute-done((bf16[512,256]{1,0:T(8,128)(2,1)S(1)}, bf16[512,256]{1,0:T(8,128)(2,1)S(1)}, u32[]{:S(2)}, u32[]{:S(2)}) %collective-permute-start.26) | collective-permute-done | bytes 262176 | tf_op jit(solution)/shard_map/ppermute | solution.py:294
  41.9 1.7 %collective-permute-start.27 = (bf16[512,256]{1,0:T(8,128)(2,1)S(1)}, bf16[512,256]{1,0:T(8,128)(2,1)S(1)}, u32[]{:S(2)}, u32[]{:S(2)}) collective-permute-start(bf16[512,256]{1,0:T(8,128)(2,1)S(1)} %add_convert_fusion.5), channel_id=1, source_target_pairs={{8,0},{16,8},{24,16},{28,24},{20,28},{12,20},{4,12},{0,4},{9,1},{1... | collective-permute-start | bytes 786440 | tf_op jit(solution)/shard_map/ppermute | solution.py:294
  44.0 1.7 %attend.19 = f32[512,256]{1,0:T(8,128)S(1)} custom-call(s32[8,8,128]{2,1,0:T(8,128)S(1)} %bitcast.16, bf16[528,256]{1,0:T(8,128)(2,1)S(1)} %collective-permute-done.8.q, bf16[64,128,512]{2,1,0:T(8,128)(2,1)S(1)} %get-tuple-element.37.cache), custom_call_target="tpu_custom_call" | custom-call | tf_op jit(solution)/shard_map/attend/pallas_call | solution.py:179
  45.8 1.8 %collective-permute-start.9 = (bf16[528,256]{1,0:T(8,128)(2,1)S(1)}, bf16[528,256]{1,0:T(8,128)(2,1)S(1)}, u32[]{:S(2)}, u32[]{:S(2)}) collective-permute-start(bf16[528,256]{1,0:T(8,128)(2,1)S(1)} %collective-permute-done.8.q), channel_id=1, source_target_pairs={{0,8},{8,16},{16,24},{24,28},{28,20},{20,12},{12,4},{4,0},{1,9},{9... | collective-permute-start | bytes 811016 | tf_op jit(solution)/shard_map/ppermute | solution.py:278
  47.6 1.7 %attend.20 = f32[512,256]{1,0:T(8,128)S(1)} custom-call(s32[8,8,128]{2,1,0:T(8,128)S(1)} %bitcast.17, bf16[528,256]{1,0:T(8,128)(2,1)S(1)} %collective-permute-done.5.q, bf16[64,128,512]{2,1,0:T(8,128)(2,1)S(1)} %get-tuple-element.37.cache), custom_call_target="tpu_custom_call" | custom-call | tf_op jit(solution)/shard_map/attend/pallas_call | solution.py:179
  49.3 1.7 %collective-permute-start.6 = (bf16[528,256]{1,0:T(8,128)(2,1)S(1)}, bf16[528,256]{1,0:T(8,128)(2,1)S(1)}, u32[]{:S(2)}, u32[]{:S(2)}) collective-permute-start(bf16[528,256]{1,0:T(8,128)(2,1)S(1)} %collective-permute-done.5.q), channel_id=1, source_target_pairs={{8,0},{16,8},{24,16},{28,24},{20,28},{12,20},{4,12},{0,4},{9,1},{1... | collective-permute-start | bytes 811016 | tf_op jit(solution)/shard_map/ppermute | solution.py:278
  51.0 2.2 %collective-permute-done.27 = bf16[512,256]{1,0:T(8,128)(2,1)S(1)} collective-permute-done((bf16[512,256]{1,0:T(8,128)(2,1)S(1)}, bf16[512,256]{1,0:T(8,128)(2,1)S(1)}, u32[]{:S(2)}, u32[]{:S(2)}) %collective-permute-start.27) | collective-permute-done | bytes 262176 | tf_op jit(solution)/shard_map/ppermute | solution.py:294
  53.3 1.7 %collective-permute-start.28 = (bf16[512,256]{1,0:T(8,128)(2,1)S(1)}, bf16[512,256]{1,0:T(8,128)(2,1)S(1)}, u32[]{:S(2)}, u32[]{:S(2)}) collective-permute-start(bf16[512,256]{1,0:T(8,128)(2,1)S(1)} %add_convert_fusion.4), channel_id=1, source_target_pairs={{8,0},{16,8},{24,16},{28,24},{20,28},{12,20},{4,12},{0,4},{9,1},{1... | collective-permute-start | bytes 786440 | tf_op jit(solution)/shard_map/ppermute | solution.py:294
  55.7 1.7 %attend.21.own = f32[512,256]{1,0:T(8,128)S(1)} custom-call(s32[8,8,128]{2,1,0:T(8,128)S(1)} %bitcast.18, bf16[528,256]{1,0:T(8,128)(2,1)S(1)} %queries.3.q, bf16[64,128,512]{2,1,0:T(8,128)(2,1)S(1)} %get-tuple-element.37.cache), custom_call_target="tpu_custom_call" | custom-call | tf_op jit(solution)/shard_map/attend/pallas_call | solution.py:179
  57.4 1.7 %attend.22 = f32[512,256]{1,0:T(8,128)S(1)} custom-call(s32[8,8,128]{2,1,0:T(8,128)S(1)} %bitcast.19, bf16[528,256]{1,0:T(8,128)(2,1)S(1)} %collective-permute-done.9.q, bf16[64,128,512]{2,1,0:T(8,128)(2,1)S(1)} %get-tuple-element.37.cache), custom_call_target="tpu_custom_call" | custom-call | tf_op jit(solution)/shard_map/attend/pallas_call | solution.py:179
  59.1 1.8 %collective-permute-start.10 = (bf16[528,256]{1,0:T(8,128)(2,1)S(1)}, bf16[528,256]{1,0:T(8,128)(2,1)S(1)}, u32[]{:S(2)}, u32[]{:S(2)}) collective-permute-start(bf16[528,256]{1,0:T(8,128)(2,1)S(1)} %collective-permute-done.9.q), channel_id=1, source_target_pairs={{0,8},{8,16},{16,24},{24,28},{28,20},{20,12},{12,4},{4,0},{1,9},{9... | collective-permute-start | bytes 811016 | tf_op jit(solution)/shard_map/ppermute | solution.py:278
  60.9 1.7 %attend.23 = f32[512,256]{1,0:T(8,128)S(1)} custom-call(s32[8,8,128]{2,1,0:T(8,128)S(1)} %bitcast.20, bf16[528,256]{1,0:T(8,128)(2,1)S(1)} %collective-permute-done.6.q, bf16[64,128,512]{2,1,0:T(8,128)(2,1)S(1)} %get-tuple-element.37.cache), custom_call_target="tpu_custom_call" | custom-call | tf_op jit(solution)/shard_map/attend/pallas_call | solution.py:179
  63.0 1.6 %collective-permute-done.28 = bf16[512,256]{1,0:T(8,128)(2,1)S(1)} collective-permute-done((bf16[512,256]{1,0:T(8,128)(2,1)S(1)}, bf16[512,256]{1,0:T(8,128)(2,1)S(1)}, u32[]{:S(2)}, u32[]{:S(2)}) %collective-permute-start.28) | collective-permute-done | bytes 262176 | tf_op jit(solution)/shard_map/ppermute | solution.py:294
  64.7 1.7 %collective-permute-start.29 = (bf16[512,256]{1,0:T(8,128)(2,1)S(1)}, bf16[512,256]{1,0:T(8,128)(2,1)S(1)}, u32[]{:S(2)}, u32[]{:S(2)}) collective-permute-start(bf16[512,256]{1,0:T(8,128)(2,1)S(1)} %add_convert_fusion.3), channel_id=1, source_target_pairs={{8,0},{16,8},{24,16},{28,24},{20,28},{12,20},{4,12},{0,4},{9,1},{1... | collective-permute-start | bytes 786440 | tf_op jit(solution)/shard_map/ppermute | solution.py:294
  66.9 1.7 %attend.24.own = f32[512,256]{1,0:T(8,128)S(1)} custom-call(s32[8,8,128]{2,1,0:T(8,128)S(1)} %bitcast.21, bf16[528,256]{1,0:T(8,128)(2,1)S(1)} %queries.2.q, bf16[64,128,512]{2,1,0:T(8,128)(2,1)S(1)} %get-tuple-element.37.cache), custom_call_target="tpu_custom_call" | custom-call | tf_op jit(solution)/shard_map/attend/pallas_call | solution.py:179
  68.6 1.7 %attend.25 = f32[512,256]{1,0:T(8,128)S(1)} custom-call(s32[8,8,128]{2,1,0:T(8,128)S(1)} %bitcast.22, bf16[528,256]{1,0:T(8,128)(2,1)S(1)} %collective-permute-done.10.q, bf16[64,128,512]{2,1,0:T(8,128)(2,1)S(1)} %get-tuple-element.37.cache), custom_call_target="tpu_custom_call" | custom-call | tf_op jit(solution)/shard_map/attend/pallas_call | solution.py:179
  70.4 1.8 %collective-permute-start.11 = (bf16[528,256]{1,0:T(8,128)(2,1)S(1)}, bf16[528,256]{1,0:T(8,128)(2,1)S(1)}, u32[]{:S(2)}, u32[]{:S(2)}) collective-permute-start(bf16[528,256]{1,0:T(8,128)(2,1)S(1)} %collective-permute-done.10.q), channel_id=1, source_target_pairs={{0,8},{8,16},{16,24},{24,28},{28,20},{20,12},{12,4},{4,0},{1,9},{9... | collective-permute-start | bytes 811016 | tf_op jit(solution)/shard_map/ppermute | solution.py:278
  72.2 1.7 %attend.26 = f32[512,256]{1,0:T(8,128)S(1)} custom-call(s32[8,8,128]{2,1,0:T(8,128)S(1)} %bitcast.23, bf16[528,256]{1,0:T(8,128)(2,1)S(1)} %collective-permute-done.14.q, bf16[64,128,512]{2,1,0:T(8,128)(2,1)S(1)} %get-tuple-element.37.cache), custom_call_target="tpu_custom_call" | custom-call | tf_op jit(solution)/shard_map/attend/pallas_call | solution.py:179
  74.3 2.1 %collective-permute-done.29 = bf16[512,256]{1,0:T(8,128)(2,1)S(1)} collective-permute-done((bf16[512,256]{1,0:T(8,128)(2,1)S(1)}, bf16[512,256]{1,0:T(8,128)(2,1)S(1)}, u32[]{:S(2)}, u32[]{:S(2)}) %collective-permute-start.29) | collective-permute-done | bytes 262176 | tf_op jit(solution)/shard_map/ppermute | solution.py:294
  76.4 1.8 %collective-permute-start.30 = (bf16[512,256]{1,0:T(8,128)(2,1)S(1)}, bf16[512,256]{1,0:T(8,128)(2,1)S(1)}, u32[]{:S(2)}, u32[]{:S(2)}) collective-permute-start(bf16[512,256]{1,0:T(8,128)(2,1)S(1)} %add_convert_fusion.2), channel_id=1, source_target_pairs={{8,0},{16,8},{24,16},{28,24},{20,28},{12,20},{4,12},{0,4},{9,1},{1... | collective-permute-start | bytes 786440 | tf_op jit(solution)/shard_map/ppermute | solution.py:294
  79.4 1.7 %attend.27 = f32[512,256]{1,0:T(8,128)S(1)} custom-call(s32[8,8,128]{2,1,0:T(8,128)S(1)} %bitcast.24, bf16[528,256]{1,0:T(8,128)(2,1)S(1)} %collective-permute-done.11.q, bf16[64,128,512]{2,1,0:T(8,128)(2,1)S(1)} %get-tuple-element.37.cache), custom_call_target="tpu_custom_call" | custom-call | tf_op jit(solution)/shard_map/attend/pallas_call | solution.py:179
  81.2 2.4 %collective-permute-start.12 = (bf16[528,256]{1,0:T(8,128)(2,1)S(1)}, bf16[528,256]{1,0:T(8,128)(2,1)S(1)}, u32[]{:S(2)}, u32[]{:S(2)}) collective-permute-start(bf16[528,256]{1,0:T(8,128)(2,1)S(1)} %collective-permute-done.11.q), channel_id=1, source_target_pairs={{0,8},{8,16},{16,24},{24,28},{28,20},{20,12},{12,4},{4,0},{1,9},{9... | collective-permute-start | bytes 811016 | tf_op jit(solution)/shard_map/ppermute | solution.py:278
  83.6 1.7 %attend.28 = f32[512,256]{1,0:T(8,128)S(1)} custom-call(s32[8,8,128]{2,1,0:T(8,128)S(1)} %bitcast.25, bf16[528,256]{1,0:T(8,128)(2,1)S(1)} %collective-permute-done.15.q, bf16[64,128,512]{2,1,0:T(8,128)(2,1)S(1)} %get-tuple-element.37.cache), custom_call_target="tpu_custom_call" | custom-call | tf_op jit(solution)/shard_map/attend/pallas_call | solution.py:179
  85.6 3.0 %collective-permute-done.30 = bf16[512,256]{1,0:T(8,128)(2,1)S(1)} collective-permute-done((bf16[512,256]{1,0:T(8,128)(2,1)S(1)}, bf16[512,256]{1,0:T(8,128)(2,1)S(1)}, u32[]{:S(2)}, u32[]{:S(2)}) %collective-permute-start.30) | collective-permute-done | bytes 262176 | tf_op jit(solution)/shard_map/ppermute | solution.py:294
  90.9 1.7 %attend.29 = f32[512,256]{1,0:T(8,128)S(1)} custom-call(s32[8,8,128]{2,1,0:T(8,128)S(1)} %bitcast.26, bf16[528,256]{1,0:T(8,128)(2,1)S(1)} %collective-permute-done.12.q, bf16[64,128,512]{2,1,0:T(8,128)(2,1)S(1)} %get-tuple-element.37.cache), custom_call_target="tpu_custom_call" | custom-call | tf_op jit(solution)/shard_map/attend/pallas_call | solution.py:179
  92.6 2.1 %collective-permute-start.13 = (bf16[528,256]{1,0:T(8,128)(2,1)S(1)}, bf16[528,256]{1,0:T(8,128)(2,1)S(1)}, u32[]{:S(2)}, u32[]{:S(2)}) collective-permute-start(bf16[528,256]{1,0:T(8,128)(2,1)S(1)} %collective-permute-done.12.q), channel_id=1, source_target_pairs={{0,8},{8,16},{16,24},{24,28},{28,20},{20,12},{12,4},{4,0},{1,9},{9... | collective-permute-start | bytes 811016 | tf_op jit(solution)/shard_map/ppermute | solution.py:278
  94.8 1.7 %attend.30 = f32[512,256]{1,0:T(8,128)S(1)} custom-call(s32[8,8,128]{2,1,0:T(8,128)S(1)} %bitcast.27, bf16[528,256]{1,0:T(8,128)(2,1)S(1)} %collective-permute-done.16.q, bf16[64,128,512]{2,1,0:T(8,128)(2,1)S(1)} %get-tuple-element.37.cache), custom_call_target="tpu_custom_call" | custom-call | tf_op jit(solution)/shard_map/attend/pallas_call | solution.py:179
  100.3 1.9 %collective-permute-done.13.q = bf16[528,256]{1,0:T(8,128)(2,1)S(1)} collective-permute-done((bf16[528,256]{1,0:T(8,128)(2,1)S(1)}, bf16[528,256]{1,0:T(8,128)(2,1)S(1)}, u32[]{:S(2)}, u32[]{:S(2)}) %collective-permute-start.13) | collective-permute-done | bytes 270368 | tf_op jit(solution)/shard_map/ppermute | solution.py:278
  102.3 1.7 %attend.31 = f32[512,256]{1,0:T(8,128)S(1)} custom-call(s32[8,8,128]{2,1,0:T(8,128)S(1)} %bitcast.28, bf16[528,256]{1,0:T(8,128)(2,1)S(1)} %collective-permute-done.13.q, bf16[64,128,512]{2,1,0:T(8,128)(2,1)S(1)} %get-tuple-element.37.cache), custom_call_target="tpu_custom_call" | custom-call | tf_op jit(solution)/shard_map/attend/pallas_call | solution.py:179
  104.7 1.8 %collective-permute-done.22 = bf16[512,256]{1,0:T(8,128)(2,1)S(1)} collective-permute-done((bf16[512,256]{1,0:T(8,128)(2,1)S(1)}, bf16[512,256]{1,0:T(8,128)(2,1)S(1)}, u32[]{:S(2)}, u32[]{:S(2)}) %collective-permute-start.22) | collective-permute-done | bytes 262176 | tf_op jit(solution)/shard_map/ppermute | solution.py:294
  108.3 5.3 %collective-permute-done.23.arrived = bf16[512,256]{1,0:T(8,128)(2,1)S(1)} collective-permute-done((bf16[512,256]{1,0:T(8,128)(2,1)S(1)}, bf16[512,256]{1,0:T(8,128)(2,1)S(1)}, u32[]{:S(2)}, u32[]{:S(2)}) %collective-permute-start.23) | collective-permute-done | bytes 262176 | tf_op jit(solution)/shard_map/ppermute | solution.py:294
  114.3 1.8 %collective-permute-start.34 = (bf16[1,512,256]{2,1,0:T(8,128)(2,1)S(1)}, bf16[1,512,256]{2,1,0:T(8,128)(2,1)S(1)}, u32[]{:S(2)}, u32[]{:S(2)}) collective-permute-start(bf16[1,512,256]{2,1,0:T(8,128)(2,1)S(1)} %slice.52), channel_id=1, source_target_pairs={{0,2},{1,3},{2,0},{3,1},{4,6},{5,7},{6,4},{7,5},{8,10},{9,11},{10,... | collective-permute-start | bytes 786440 | tf_op jit(solution)/shard_map/ppermute | solution.py:243
  116.2 1.7 %collective-permute-start.25 = (bf16[1,512,256]{2,1,0:T(8,128)(2,1)S(1)}, bf16[1,512,256]{2,1,0:T(8,128)(2,1)S(1)}, u32[]{:S(2)}, u32[]{:S(2)}) collective-permute-start(bf16[1,512,256]{2,1,0:T(8,128)(2,1)S(1)} %slice.53), channel_id=1, source_target_pairs={{0,2},{1,3},{2,0},{3,1},{4,6},{5,7},{6,4},{7,5},{8,10},{9,11},{10,... | collective-permute-start | bytes 786440 | tf_op jit(solution)/shard_map/ppermute | solution.py:243
  118.0 5.5 %collective-permute-done.34 = bf16[1,512,256]{2,1,0:T(8,128)(2,1)S(1)} collective-permute-done((bf16[1,512,256]{2,1,0:T(8,128)(2,1)S(1)}, bf16[1,512,256]{2,1,0:T(8,128)(2,1)S(1)}, u32[]{:S(2)}, u32[]{:S(2)}) %collective-permute-start.34) | collective-permute-done | bytes 262176 | tf_op jit(solution)/shard_map/ppermute | solution.py:243
  123.5 5.2 %collective-permute-done.25 = bf16[1,512,256]{2,1,0:T(8,128)(2,1)S(1)} collective-permute-done((bf16[1,512,256]{2,1,0:T(8,128)(2,1)S(1)}, bf16[1,512,256]{2,1,0:T(8,128)(2,1)S(1)}, u32[]{:S(2)}, u32[]{:S(2)}) %collective-permute-start.25) | collective-permute-done | bytes 262176 | tf_op jit(solution)/shard_map/ppermute | solution.py:243
  (84 shorter events, 21.5 us)
Async XLA Ops:
  0.0 5.2 %collective-permute-start = (bf16[1024,256]{1,0:T(8,128)(2,1)}, bf16[1024,256]{1,0:T(8,128)(2,1)S(1)}, u32[]{:S(2)}, u32[]{:S(2)}) collective-permute-start(bf16[1024,256]{1,0:T(8,128)(2,1)} %feats.1), channel_id=1, source_target_pairs={{0,1},{1,0},{2,3},{3,2},{4,5},{5,4},{6,7},{7,6},{8,9},{9,8},{10,11... | collective-permute-start | bytes 1572872 | tf_op jit(solution)/shard_map/ppermute | solution.py:243
  0.5 15.3 %collective-permute-start.1 = (bf16[1024,256]{1,0:T(8,128)(2,1)}, bf16[1024,256]{1,0:T(8,128)(2,1)S(1)}, u32[]{:S(2)}, u32[]{:S(2)}) collective-permute-start(bf16[1024,256]{1,0:T(8,128)(2,1)} %feats.1), channel_id=1, source_target_pairs={{0,2},{1,3},{2,0},{3,1},{4,6},{5,7},{6,4},{7,5},{8,10},{9,11},{10,... | collective-permute-start | bytes 1572872 | tf_op jit(solution)/shard_map/ppermute | solution.py:243
  5.3 1.0 copy-start.1
  6.3 0.8 copy-start.3
  7.1 0.7 copy-start.4
  15.8 1.9 %collective-permute-start.2 = (bf16[1024,256]{1,0:T(8,128)(2,1)S(1)}, bf16[1024,256]{1,0:T(8,128)(2,1)S(1)}, u32[]{:S(2)}, u32[]{:S(2)}) collective-permute-start(bf16[1024,256]{1,0:T(8,128)(2,1)S(1)} %collective-permute-done.1.refs_0_), channel_id=1, source_target_pairs={{0,1},{1,0},{2,3},{3,2},{4,5},{5,4},{6,7},{7,6},{8,9},{9,8},{10,11... | collective-permute-start | bytes 1572872 | tf_op jit(solution)/shard_map/ppermute | solution.py:243
  18.1 8.6 %collective-permute-start.3 = (bf16[528,256]{1,0:T(8,128)(2,1)S(1)}, bf16[528,256]{1,0:T(8,128)(2,1)S(1)}, u32[]{:S(2)}, u32[]{:S(2)}) collective-permute-start(bf16[528,256]{1,0:T(8,128)(2,1)S(1)} %queries.3.q), channel_id=1, source_target_pairs={{8,0},{16,8},{24,16},{28,24},{20,28},{12,20},{4,12},{0,4},{9,1},{1... | collective-permute-start | bytes 811016 | tf_op jit(solution)/shard_map/ppermute | solution.py:278
  20.4 11.5 %collective-permute-start.7 = (bf16[528,256]{1,0:T(8,128)(2,1)S(1)}, bf16[528,256]{1,0:T(8,128)(2,1)S(1)}, u32[]{:S(2)}, u32[]{:S(2)}) collective-permute-start(bf16[528,256]{1,0:T(8,128)(2,1)S(1)} %queries.2.q), channel_id=1, source_target_pairs={{0,8},{8,16},{16,24},{24,28},{28,20},{20,12},{12,4},{4,0},{1,9},{9... | collective-permute-start | bytes 811016 | tf_op jit(solution)/shard_map/ppermute | solution.py:278
  26.8 9.4 %collective-permute-start.4 = (bf16[528,256]{1,0:T(8,128)(2,1)S(1)}, bf16[528,256]{1,0:T(8,128)(2,1)S(1)}, u32[]{:S(2)}, u32[]{:S(2)}) collective-permute-start(bf16[528,256]{1,0:T(8,128)(2,1)S(1)} %collective-permute-done.3.q), channel_id=1, source_target_pairs={{8,0},{16,8},{24,16},{28,24},{20,28},{12,20},{4,12},{0,4},{9,1},{1... | collective-permute-start | bytes 811016 | tf_op jit(solution)/shard_map/ppermute | solution.py:278
  30.2 11.6 %collective-permute-start.26 = (bf16[512,256]{1,0:T(8,128)(2,1)S(1)}, bf16[512,256]{1,0:T(8,128)(2,1)S(1)}, u32[]{:S(2)}, u32[]{:S(2)}) collective-permute-start(bf16[512,256]{1,0:T(8,128)(2,1)S(1)} %convert_element_type.125), channel_id=1, source_target_pairs={{8,0},{16,8},{24,16},{28,24},{20,28},{12,20},{4,12},{0,4},{9,1},{1... | collective-permute-start | bytes 786440 | tf_op jit(solution)/shard_map/ppermute | solution.py:294
  33.6 10.5 %collective-permute-start.8 = (bf16[528,256]{1,0:T(8,128)(2,1)S(1)}, bf16[528,256]{1,0:T(8,128)(2,1)S(1)}, u32[]{:S(2)}, u32[]{:S(2)}) collective-permute-start(bf16[528,256]{1,0:T(8,128)(2,1)S(1)} %collective-permute-done.7.q), channel_id=1, source_target_pairs={{0,8},{8,16},{16,24},{24,28},{28,20},{20,12},{12,4},{4,0},{1,9},{9... | collective-permute-start | bytes 811016 | tf_op jit(solution)/shard_map/ppermute | solution.py:278
  37.9 9.7 %collective-permute-start.5 = (bf16[528,256]{1,0:T(8,128)(2,1)S(1)}, bf16[528,256]{1,0:T(8,128)(2,1)S(1)}, u32[]{:S(2)}, u32[]{:S(2)}) collective-permute-start(bf16[528,256]{1,0:T(8,128)(2,1)S(1)} %collective-permute-done.4.q), channel_id=1, source_target_pairs={{8,0},{16,8},{24,16},{28,24},{20,28},{12,20},{4,12},{0,4},{9,1},{1... | collective-permute-start | bytes 811016 | tf_op jit(solution)/shard_map/ppermute | solution.py:278
  41.9 11.4 %collective-permute-start.27 = (bf16[512,256]{1,0:T(8,128)(2,1)S(1)}, bf16[512,256]{1,0:T(8,128)(2,1)S(1)}, u32[]{:S(2)}, u32[]{:S(2)}) collective-permute-start(bf16[512,256]{1,0:T(8,128)(2,1)S(1)} %add_convert_fusion.5), channel_id=1, source_target_pairs={{8,0},{16,8},{24,16},{28,24},{20,28},{12,20},{4,12},{0,4},{9,1},{1... | collective-permute-start | bytes 786440 | tf_op jit(solution)/shard_map/ppermute | solution.py:294
  43.6 11.4 %collective-permute-start.17 = (bf16[512,256]{1,0:T(8,128)(2,1)S(1)}, bf16[512,256]{1,0:T(8,128)(2,1)S(1)}, u32[]{:S(2)}, u32[]{:S(2)}) collective-permute-start(bf16[512,256]{1,0:T(8,128)(2,1)S(1)} %convert_element_type.108), channel_id=1, source_target_pairs={{0,8},{8,16},{16,24},{24,28},{28,20},{20,12},{12,4},{4,0},{1,9},{9... | collective-permute-start | bytes 786440 | tf_op jit(solution)/shard_map/ppermute | solution.py:294
  45.8 11.6 %collective-permute-start.9 = (bf16[528,256]{1,0:T(8,128)(2,1)S(1)}, bf16[528,256]{1,0:T(8,128)(2,1)S(1)}, u32[]{:S(2)}, u32[]{:S(2)}) collective-permute-start(bf16[528,256]{1,0:T(8,128)(2,1)S(1)} %collective-permute-done.8.q), channel_id=1, source_target_pairs={{0,8},{8,16},{16,24},{24,28},{28,20},{20,12},{12,4},{4,0},{1,9},{9... | collective-permute-start | bytes 811016 | tf_op jit(solution)/shard_map/ppermute | solution.py:278
  49.3 11.6 %collective-permute-start.6 = (bf16[528,256]{1,0:T(8,128)(2,1)S(1)}, bf16[528,256]{1,0:T(8,128)(2,1)S(1)}, u32[]{:S(2)}, u32[]{:S(2)}) collective-permute-start(bf16[528,256]{1,0:T(8,128)(2,1)S(1)} %collective-permute-done.5.q), channel_id=1, source_target_pairs={{8,0},{16,8},{24,16},{28,24},{20,28},{12,20},{4,12},{0,4},{9,1},{1... | collective-permute-start | bytes 811016 | tf_op jit(solution)/shard_map/ppermute | solution.py:278
  53.3 11.4 %collective-permute-start.28 = (bf16[512,256]{1,0:T(8,128)(2,1)S(1)}, bf16[512,256]{1,0:T(8,128)(2,1)S(1)}, u32[]{:S(2)}, u32[]{:S(2)}) collective-permute-start(bf16[512,256]{1,0:T(8,128)(2,1)S(1)} %add_convert_fusion.4), channel_id=1, source_target_pairs={{8,0},{16,8},{24,16},{28,24},{20,28},{12,20},{4,12},{0,4},{9,1},{1... | collective-permute-start | bytes 786440 | tf_op jit(solution)/shard_map/ppermute | solution.py:294
  55.1 11.4 %collective-permute-start.18 = (bf16[512,256]{1,0:T(8,128)(2,1)S(1)}, bf16[512,256]{1,0:T(8,128)(2,1)S(1)}, u32[]{:S(2)}, u32[]{:S(2)}) collective-permute-start(bf16[512,256]{1,0:T(8,128)(2,1)S(1)} %add_convert_fusion.11), channel_id=1, source_target_pairs={{0,8},{8,16},{16,24},{24,28},{28,20},{20,12},{12,4},{4,0},{1,9},{9... | collective-permute-start | bytes 786440 | tf_op jit(solution)/shard_map/ppermute | solution.py:294
  59.1 9.5 %collective-permute-start.10 = (bf16[528,256]{1,0:T(8,128)(2,1)S(1)}, bf16[528,256]{1,0:T(8,128)(2,1)S(1)}, u32[]{:S(2)}, u32[]{:S(2)}) collective-permute-start(bf16[528,256]{1,0:T(8,128)(2,1)S(1)} %collective-permute-done.9.q), channel_id=1, source_target_pairs={{0,8},{8,16},{16,24},{24,28},{28,20},{20,12},{12,4},{4,0},{1,9},{9... | collective-permute-start | bytes 811016 | tf_op jit(solution)/shard_map/ppermute | solution.py:278
  62.7 9.5 %collective-permute-start.14 = (bf16[528,256]{1,0:T(8,128)(2,1)S(1)}, bf16[528,256]{1,0:T(8,128)(2,1)S(1)}, u32[]{:S(2)}, u32[]{:S(2)}) collective-permute-start(bf16[528,256]{1,0:T(8,128)(2,1)S(1)} %collective-permute-done.6.q), channel_id=1, source_target_pairs={{8,0},{16,8},{24,16},{28,24},{20,28},{12,20},{4,12},{0,4},{9,1},{1... | collective-permute-start | bytes 811016 | tf_op jit(solution)/shard_map/ppermute | solution.py:278
  64.7 11.6 %collective-permute-start.29 = (bf16[512,256]{1,0:T(8,128)(2,1)S(1)}, bf16[512,256]{1,0:T(8,128)(2,1)S(1)}, u32[]{:S(2)}, u32[]{:S(2)}) collective-permute-start(bf16[512,256]{1,0:T(8,128)(2,1)S(1)} %add_convert_fusion.3), channel_id=1, source_target_pairs={{8,0},{16,8},{24,16},{28,24},{20,28},{12,20},{4,12},{0,4},{9,1},{1... | collective-permute-start | bytes 786440 | tf_op jit(solution)/shard_map/ppermute | solution.py:294
  66.5 11.7 %collective-permute-start.19 = (bf16[512,256]{1,0:T(8,128)(2,1)S(1)}, bf16[512,256]{1,0:T(8,128)(2,1)S(1)}, u32[]{:S(2)}, u32[]{:S(2)}) collective-permute-start(bf16[512,256]{1,0:T(8,128)(2,1)S(1)} %add_convert_fusion.10), channel_id=1, source_target_pairs={{0,8},{8,16},{16,24},{24,28},{28,20},{20,12},{12,4},{4,0},{1,9},{9... | collective-permute-start | bytes 786440 | tf_op jit(solution)/shard_map/ppermute | solution.py:294
  70.4 9.1 %collective-permute-start.11 = (bf16[528,256]{1,0:T(8,128)(2,1)S(1)}, bf16[528,256]{1,0:T(8,128)(2,1)S(1)}, u32[]{:S(2)}, u32[]{:S(2)}) collective-permute-start(bf16[528,256]{1,0:T(8,128)(2,1)S(1)} %collective-permute-done.10.q), channel_id=1, source_target_pairs={{0,8},{8,16},{16,24},{24,28},{28,20},{20,12},{12,4},{4,0},{1,9},{9... | collective-permute-start | bytes 811016 | tf_op jit(solution)/shard_map/ppermute | solution.py:278
  73.9 9.7 %collective-permute-start.15 = (bf16[528,256]{1,0:T(8,128)(2,1)S(1)}, bf16[528,256]{1,0:T(8,128)(2,1)S(1)}, u32[]{:S(2)}, u32[]{:S(2)}) collective-permute-start(bf16[528,256]{1,0:T(8,128)(2,1)S(1)} %collective-permute-done.14.q), channel_id=1, source_target_pairs={{8,0},{16,8},{24,16},{28,24},{20,28},{12,20},{4,12},{0,4},{9,1},{1... | collective-permute-start | bytes 811016 | tf_op jit(solution)/shard_map/ppermute | solution.py:278
  76.4 12.2 %collective-permute-start.30 = (bf16[512,256]{1,0:T(8,128)(2,1)S(1)}, bf16[512,256]{1,0:T(8,128)(2,1)S(1)}, u32[]{:S(2)}, u32[]{:S(2)}) collective-permute-start(bf16[512,256]{1,0:T(8,128)(2,1)S(1)} %add_convert_fusion.2), channel_id=1, source_target_pairs={{8,0},{16,8},{24,16},{28,24},{20,28},{12,20},{4,12},{0,4},{9,1},{1... | collective-permute-start | bytes 786440 | tf_op jit(solution)/shard_map/ppermute | solution.py:294
  78.2 11.3 %collective-permute-start.20 = (bf16[512,256]{1,0:T(8,128)(2,1)S(1)}, bf16[512,256]{1,0:T(8,128)(2,1)S(1)}, u32[]{:S(2)}, u32[]{:S(2)}) collective-permute-start(bf16[512,256]{1,0:T(8,128)(2,1)S(1)} %add_convert_fusion.9), channel_id=1, source_target_pairs={{0,8},{8,16},{16,24},{24,28},{28,20},{20,12},{12,4},{4,0},{1,9},{9... | collective-permute-start | bytes 786440 | tf_op jit(solution)/shard_map/ppermute | solution.py:294
  81.2 9.7 %collective-permute-start.12 = (bf16[528,256]{1,0:T(8,128)(2,1)S(1)}, bf16[528,256]{1,0:T(8,128)(2,1)S(1)}, u32[]{:S(2)}, u32[]{:S(2)}) collective-permute-start(bf16[528,256]{1,0:T(8,128)(2,1)S(1)} %collective-permute-done.11.q), channel_id=1, source_target_pairs={{0,8},{8,16},{16,24},{24,28},{28,20},{20,12},{12,4},{4,0},{1,9},{9... | collective-permute-start | bytes 811016 | tf_op jit(solution)/shard_map/ppermute | solution.py:278
  85.3 9.5 %collective-permute-start.16 = (bf16[528,256]{1,0:T(8,128)(2,1)S(1)}, bf16[528,256]{1,0:T(8,128)(2,1)S(1)}, u32[]{:S(2)}, u32[]{:S(2)}) collective-permute-start(bf16[528,256]{1,0:T(8,128)(2,1)S(1)} %collective-permute-done.15.q), channel_id=1, source_target_pairs={{8,0},{16,8},{24,16},{28,24},{20,28},{12,20},{4,12},{0,4},{9,1},{1... | collective-permute-start | bytes 811016 | tf_op jit(solution)/shard_map/ppermute | solution.py:278
  88.7 8.6 %collective-permute-start.31 = (bf16[512,256]{1,0:T(8,128)(2,1)S(1)}, bf16[512,256]{1,0:T(8,128)(2,1)S(1)}, u32[]{:S(2)}, u32[]{:S(2)}) collective-permute-start(bf16[512,256]{1,0:T(8,128)(2,1)S(1)} %add_convert_fusion.1), channel_id=1, source_target_pairs={{8,0},{16,8},{24,16},{28,24},{20,28},{12,20},{4,12},{0,4},{9,1},{1... | collective-permute-start | bytes 786440 | tf_op jit(solution)/shard_map/ppermute | solution.py:294
  89.6 9.3 %collective-permute-start.21 = (bf16[512,256]{1,0:T(8,128)(2,1)S(1)}, bf16[512,256]{1,0:T(8,128)(2,1)S(1)}, u32[]{:S(2)}, u32[]{:S(2)}) collective-permute-start(bf16[512,256]{1,0:T(8,128)(2,1)S(1)} %add_convert_fusion.8), channel_id=1, source_target_pairs={{0,8},{8,16},{16,24},{24,28},{28,20},{20,12},{12,4},{4,0},{1,9},{9... | collective-permute-start | bytes 786440 | tf_op jit(solution)/shard_map/ppermute | solution.py:294
  92.6 9.6 %collective-permute-start.13 = (bf16[528,256]{1,0:T(8,128)(2,1)S(1)}, bf16[528,256]{1,0:T(8,128)(2,1)S(1)}, u32[]{:S(2)}, u32[]{:S(2)}) collective-permute-start(bf16[528,256]{1,0:T(8,128)(2,1)S(1)} %collective-permute-done.12.q), channel_id=1, source_target_pairs={{0,8},{8,16},{16,24},{24,28},{28,20},{20,12},{12,4},{4,0},{1,9},{9... | collective-permute-start | bytes 811016 | tf_op jit(solution)/shard_map/ppermute | solution.py:278
  96.5 7.6 %copy-start = (bf16[256,1024]{1,0:T(8,128)(2,1)S(1)}, bf16[256,1024]{1,0:T(8,128)(2,1)}, u32[]{:S(2)}) copy-start(bf16[256,1024]{1,0:T(8,128)(2,1)} %w_out.3) | copy-start | bytes 1572868
  97.3 6.8 %collective-permute-start.32 = (bf16[512,256]{1,0:T(8,128)(2,1)S(1)}, bf16[512,256]{1,0:T(8,128)(2,1)S(1)}, u32[]{:S(2)}, u32[]{:S(2)}) collective-permute-start(bf16[512,256]{1,0:T(8,128)(2,1)S(1)} %add_convert_fusion), channel_id=1, source_target_pairs={{8,0},{16,8},{24,16},{28,24},{20,28},{12,20},{4,12},{0,4},{9,1},{1... | collective-permute-start | bytes 786440 | tf_op jit(solution)/shard_map/ppermute | solution.py:294
  99.0 7.5 %collective-permute-start.22 = (bf16[512,256]{1,0:T(8,128)(2,1)S(1)}, bf16[512,256]{1,0:T(8,128)(2,1)S(1)}, u32[]{:S(2)}, u32[]{:S(2)}) collective-permute-start(bf16[512,256]{1,0:T(8,128)(2,1)S(1)} %add_convert_fusion.7), channel_id=1, source_target_pairs={{0,8},{8,16},{16,24},{24,28},{28,20},{20,12},{12,4},{4,0},{1,9},{9... | collective-permute-start | bytes 786440 | tf_op jit(solution)/shard_map/ppermute | solution.py:294
  104.0 24.7 %copy-start.2 = (bf16[1024,256]{1,0:T(8,128)(2,1)S(1)}, bf16[1024,256]{1,0:T(8,128)(2,1)}, u32[]{:S(2)}) copy-start(bf16[1024,256]{1,0:T(8,128)(2,1)} %feats.1) | copy-start | bytes 1572868
  104.6 9.5 %collective-permute-start.33 = (bf16[2,512,256]{2,1,0:T(8,128)(2,1)S(1)}, bf16[2,512,256]{2,1,0:T(8,128)(2,1)S(1)}, u32[]{:S(2)}, u32[]{:S(2)}) collective-permute-start(bf16[2,512,256]{2,1,0:T(8,128)(2,1)S(1)} %get-tuple-element.56), channel_id=1, source_target_pairs={{0,1},{1,0},{2,3},{3,2},{4,5},{5,4},{6,7},{7,6},{8,9},{9,8},{10,11... | collective-permute-start | bytes 1572872 | tf_op jit(solution)/shard_map/ppermute | solution.py:243
  106.6 7.0 %collective-permute-start.23 = (bf16[512,256]{1,0:T(8,128)(2,1)S(1)}, bf16[512,256]{1,0:T(8,128)(2,1)S(1)}, u32[]{:S(2)}, u32[]{:S(2)}) collective-permute-start(bf16[512,256]{1,0:T(8,128)(2,1)S(1)} %add_convert_fusion.6), channel_id=1, source_target_pairs={{0,8},{8,16},{16,24},{24,28},{28,20},{20,12},{12,4},{4,0},{1,9},{9... | collective-permute-start | bytes 786440 | tf_op jit(solution)/shard_map/ppermute | solution.py:294
  114.1 2.0 %collective-permute-start.24 = (bf16[2,512,256]{2,1,0:T(8,128)(2,1)S(1)}, bf16[2,512,256]{2,1,0:T(8,128)(2,1)S(1)}, u32[]{:S(2)}, u32[]{:S(2)}) collective-permute-start(bf16[2,512,256]{2,1,0:T(8,128)(2,1)S(1)} %get-tuple-element.54), channel_id=1, source_target_pairs={{0,1},{1,0},{2,3},{3,2},{4,5},{5,4},{6,7},{7,6},{8,9},{9,8},{10,11... | collective-permute-start | bytes 1572872 | tf_op jit(solution)/shard_map/ppermute | solution.py:243
  114.3 9.2 %collective-permute-start.34 = (bf16[1,512,256]{2,1,0:T(8,128)(2,1)S(1)}, bf16[1,512,256]{2,1,0:T(8,128)(2,1)S(1)}, u32[]{:S(2)}, u32[]{:S(2)}) collective-permute-start(bf16[1,512,256]{2,1,0:T(8,128)(2,1)S(1)} %slice.52), channel_id=1, source_target_pairs={{0,2},{1,3},{2,0},{3,1},{4,6},{5,7},{6,4},{7,5},{8,10},{9,11},{10,... | collective-permute-start | bytes 786440 | tf_op jit(solution)/shard_map/ppermute | solution.py:243
  116.2 12.5 %collective-permute-start.25 = (bf16[1,512,256]{2,1,0:T(8,128)(2,1)S(1)}, bf16[1,512,256]{2,1,0:T(8,128)(2,1)S(1)}, u32[]{:S(2)}, u32[]{:S(2)}) collective-permute-start(bf16[1,512,256]{2,1,0:T(8,128)(2,1)S(1)} %slice.53), channel_id=1, source_target_pairs={{0,2},{1,3},{2,0},{3,1},{4,6},{5,7},{6,4},{7,5},{8,10},{9,11},{10,... | collective-permute-start | bytes 786440 | tf_op jit(solution)/shard_map/ppermute | solution.py:243
